TPU v7x, 128 devices: a whole 4x4x4 slice. The times are simulated.
128 devices in a mesh: dp: 32 (over x_hi, z, y), tensor: 4 (over x_lo, core).
Axes of the slice: x: 4 (x_hi: 2, x_lo: 2; x = x_hi * 2 + x_lo), y: 4, z: 4, core: 2. Of those that a mesh axis runs over, the one named last changes fastest.
Arguments:
- tokens: bfloat16 [32768, 640], P(('dp', 'tensor')), may hold values from -6 to 6
- segments: int32 [32, 1024], P('dp'), may hold values from 0 to 2, as said below
- cotangent: bfloat16 [32768, 640], P(('dp', 'tensor')), may hold values from -24 to 24
- w_query: bfloat16 [640, 1024], P('dp', 'tensor'), may hold values from -0.25 to 0.25
- w_keyval: bfloat16 [640, 512], P('dp'), may hold values from -0.25 to 0.25
- w_out: bfloat16 [1024, 640], P('tensor', 'dp'), may hold values from -0.1875 to 0.1875
- w_gate: bfloat16 [640, 2048], P('dp', 'tensor'), may hold values from -0.25 to 0.25
- w_up: bfloat16 [640, 2048], P('dp', 'tensor'), may hold values from -0.25 to 0.25
- w_down: bfloat16 [2048, 640], P('tensor', 'dp'), may hold values from -0.125 to 0.125
- gain_in: float32 [640], replicated, may hold values from 0.25 to 1.75
- gain_post_attn: float32 [640], replicated, may hold values from 0.25 to 1.75
- gain_pre_ff: float32 [640], replicated, may hold values from 0.25 to 1.75
- gain_post_ff: float32 [640], replicated, may hold values from 0.25 to 1.75
- gain_query: float32 [256], replicated, may hold values from 0.25 to 1.75
- gain_key: float32 [256], replicated, may hold values from 0.25 to 1.75
Outputs:
- output: bfloat16 [32768, 640], P(('dp', 'tensor'))
- grad_x: float32 [32768, 640], P(('dp', 'tensor'))
- grad_query: float32 [640, 1024], P('dp', 'tensor')
- grad_keyval: float32 [640, 512], P('dp')
- grad_out: float32 [1024, 640], P('tensor', 'dp')
- grad_gate: float32 [640, 2048], P('dp', 'tensor')
- grad_up: float32 [640, 2048], P('dp', 'tensor')
- grad_down: float32 [2048, 640], P('tensor', 'dp')
- grad_gain_in: float32 [640], replicated
- grad_gain_post_attn: float32 [640], replicated
- grad_gain_pre_ff: float32 [640], replicated
- grad_gain_post_ff: float32 [640], replicated
- grad_gain_query: float32 [256], replicated
- grad_gain_key: float32 [256], replicated
Inputs may be any that keep to these rules, and one draw needn't show every extreme that they name: `segments`: along each row the numbers never fall; each row holds three documents numbered 0, 1, 2, each of one token or more, where document 1 starts within the first 256 tokens and ends within the last 256.
All inputs are finite; a program needn't handle non-finite values.
Results may differ from a plain program's by a relative error of at most 0.024.
Values may be sent and summed in bfloat16 or wider, within the bound.
A program may use at most 128 MiB of HBM per device.

v0:
```python
import jax
import jax.numpy as jnp
from jax import lax
from jax.sharding import PartitionSpec as P

HD = 256
WINDOW = 512


norm_eps = 1e-06
rope_base = 10000.0


def rms_scale(array_in, gain_row):
    return (
        array_in
        * lax.rsqrt(jnp.mean(array_in * array_in, axis=-1, keepdims=True) + norm_eps)
        * gain_row
    )


def rotate_half(array_in):
    half_width = array_in.shape[-1] // 2
    return jnp.concatenate([-array_in[..., half_width:], array_in[..., :half_width]], axis=-1)


def rope_tables(position_ids, head_width):
    inv_freq = rope_base ** (-jnp.arange(0, head_width, 2).astype(jnp.float32) / head_width)
    angles = position_ids.astype(jnp.float32)[:, None] * inv_freq[None, :]
    angles = jnp.concatenate([angles, angles], axis=-1)
    return (jnp.cos(angles), jnp.sin(angles))


def segment_positions(seg_ids):
    row_index = jnp.arange(seg_ids.shape[0], dtype=jnp.int32)
    prev_ids = jnp.concatenate([seg_ids[:1] - 1, seg_ids[:-1]])
    doc_start = lax.cummax(jnp.where(seg_ids != prev_ids, row_index, 0), axis=0)
    return row_index - doc_start


def prepare(raw_rows, gain_row, cos_rows, sin_rows):
    normed = rms_scale(raw_rows, gain_row)
    return normed * cos_rows + rotate_half(normed) * sin_rows


def norm_back(array_in, gain_row, grad_rows):
    _, back_fn = jax.vjp(rms_scale, array_in, gain_row)
    return back_fn(grad_rows)


def gelu_product(gate_rows, up_rows):
    return jax.nn.gelu(gate_rows, approximate=True) * up_rows


def contract_rows(left_rows, right_rows):
    return lax.dot_general(
        left_rows, right_rows, (((0,), (0,)), ((), ())), preferred_element_type=jnp.float32
    )


def project_back(grad_rows, weight_rows):
    return lax.dot_general(
        grad_rows, weight_rows, (((1,), (1,)), ((), ())), preferred_element_type=jnp.float32
    )


def per_device(
    tokens,
    segments,
    cotangent,
    w_query,
    w_keyval,
    w_out,
    w_gate,
    w_up,
    w_down,
    gain_in,
    gain_post_attn,
    gain_pre_ff,
    gain_post_ff,
    gain_query,
    gain_key,
):
    tok_rows = tokens.shape[0]
    seq_rows = tok_rows * lax.axis_size("tensor")
    model_width = tokens.shape[1]
    heads_here = w_query.shape[1] // HD
    seg_ids = segments[0]
    positions = segment_positions(seg_ids)
    cos_rows, sin_rows = rope_tables(positions, HD)
    cos_heads = cos_rows[:, None, :]
    sin_heads = sin_rows[:, None, :]
    score_scale = HD ** (-0.5)
    q_block = min(512, seq_rows)
    key_reach = -(-WINDOW // q_block) * q_block
    key_span = min(seq_rows, q_block + key_reach)
    starts = jnp.arange(seq_rows // q_block, dtype=jnp.int32) * q_block
    x_local = tokens.astype(jnp.float32)
    attn_local = rms_scale(x_local, gain_in).astype(jnp.bfloat16)
    query_full, keyval_full, out_full = (
        lax.all_gather(w_query, "dp", axis=0, tiled=True),
        lax.all_gather(w_keyval, "dp", axis=0, tiled=True),
        lax.all_gather(w_out, "dp", axis=1, tiled=True),
    )
    attn_input = lax.all_gather(attn_local, "tensor", axis=0, tiled=True)
    query_raw = jnp.dot(attn_input, query_full, preferred_element_type=jnp.float32).reshape(
        seq_rows, heads_here, HD
    )
    keyval_raw = jnp.dot(attn_input, keyval_full, preferred_element_type=jnp.float32)
    key_raw = keyval_raw[:, :HD]
    queries = prepare(query_raw, gain_query, cos_heads, sin_heads).astype(jnp.bfloat16)
    key_rows = prepare(key_raw, gain_key, cos_rows, sin_rows).astype(jnp.bfloat16)
    values = keyval_raw[:, HD:].astype(jnp.bfloat16)

    def block_scores(first_row):
        key_start = jnp.clip(first_row - key_reach, 0, seq_rows - key_span)
        query_blk = lax.dynamic_slice_in_dim(queries, first_row, q_block, 0)
        query_index = first_row + jnp.arange(q_block, dtype=jnp.int32)
        key_index = key_start + jnp.arange(key_span, dtype=jnp.int32)
        query_seg = lax.dynamic_slice_in_dim(seg_ids, first_row, q_block, 0)
        offset = query_index[:, None] - key_index[None, :]
        allowed = (query_seg[:, None] == seg_ids[None, :]) & (offset >= 0) & (offset < WINDOW)
        scores = (
            jnp.einsum("qhd,kd->hqk", query_blk, key_rows, preferred_element_type=jnp.float32)
            * score_scale
        )
        scores = jnp.where(allowed[None], scores, -1e30)
        return (scores, query_blk, key_rows, values, key_start)

    def attend(first_row):
        scores, query_blk, key_blk, value_blk, key_start = block_scores(first_row)
        row_max = jnp.max(scores, axis=-1, keepdims=True)
        exp_scores = jnp.exp(scores - row_max)
        exp_sum = jnp.sum(exp_scores, axis=-1, keepdims=True)
        attn_probs = (exp_scores / exp_sum).astype(jnp.bfloat16)
        context_blk = jnp.einsum(
            "hqk,kd->qhd", attn_probs, value_blk, preferred_element_type=jnp.float32
        )
        return (context_blk, (row_max + jnp.log(exp_sum))[..., 0])

    context, log_total = lax.map(attend, starts)
    context_b = context.reshape(seq_rows, heads_here * HD).astype(jnp.bfloat16)
    rows_here = context_b
    attn_proj = lax.psum_scatter(
        jnp.dot(rows_here, out_full, preferred_element_type=jnp.float32),
        "tensor",
        scatter_dimension=0,
        tiled=True,
    )
    mid_rows = x_local + rms_scale(attn_proj, gain_post_attn)
    mlp_local = rms_scale(mid_rows, gain_pre_ff).astype(jnp.bfloat16)
    gate_full, up_full, down_full = (
        lax.all_gather(w_gate, "dp", axis=0, tiled=True),
        lax.all_gather(w_up, "dp", axis=0, tiled=True),
        lax.all_gather(w_down, "dp", axis=1, tiled=True),
    )
    mlp_input = lax.all_gather(mlp_local, "tensor", axis=0, tiled=True)
    gate_rows = jnp.dot(mlp_input, gate_full, preferred_element_type=jnp.float32)
    up_rows = jnp.dot(mlp_input, up_full, preferred_element_type=jnp.float32)
    hidden = gelu_product(gate_rows, up_rows).astype(jnp.bfloat16)
    rows_here = hidden
    mlp_proj = lax.psum_scatter(
        jnp.dot(rows_here, down_full, preferred_element_type=jnp.float32),
        "tensor",
        scatter_dimension=0,
        tiled=True,
    )
    output = (mid_rows + rms_scale(mlp_proj, gain_post_ff)).astype(jnp.bfloat16)
    grad_top = cotangent.astype(jnp.float32)
    d_mlp_f, grad_gain_post_ff = norm_back(mlp_proj, gain_post_ff, grad_top)
    d_mlp_all = lax.all_gather(d_mlp_f.astype(jnp.bfloat16), "tensor", axis=0, tiled=True)
    down_part = contract_rows(hidden, d_mlp_all)
    d_hidden = project_back(d_mlp_all, down_full)
    _, hidden_back = jax.vjp(gelu_product, gate_rows, up_rows)
    d_gate_f, d_up_f = hidden_back(d_hidden)
    d_gate = d_gate_f.astype(jnp.bfloat16)
    d_up = d_up_f.astype(jnp.bfloat16)
    gate_part = contract_rows(mlp_input, d_gate)
    up_part = contract_rows(mlp_input, d_up)
    d_mlp_input = lax.psum_scatter(
        project_back(d_gate, gate_full) + project_back(d_up, up_full),
        "tensor",
        scatter_dimension=0,
        tiled=True,
    )
    grad_gate, grad_up, grad_down = (
        lax.psum_scatter(
            gate_part.astype(jnp.bfloat16), "dp", scatter_dimension=0, tiled=True
        ).astype(jnp.float32),
        lax.psum_scatter(
            up_part.astype(jnp.bfloat16), "dp", scatter_dimension=0, tiled=True
        ).astype(jnp.float32),
        lax.psum_scatter(
            down_part.astype(jnp.bfloat16), "dp", scatter_dimension=1, tiled=True
        ).astype(jnp.float32),
    )
    d_pre, grad_gain_pre_ff = norm_back(mid_rows, gain_pre_ff, d_mlp_input)
    d_mid = grad_top + d_pre
    d_attn_f, grad_gain_post_attn = norm_back(attn_proj, gain_post_attn, d_mid)
    d_attn_all = lax.all_gather(d_attn_f.astype(jnp.bfloat16), "tensor", axis=0, tiled=True)
    out_part = contract_rows(context_b, d_attn_all)
    d_context = (
        project_back(d_attn_all, out_full).astype(jnp.bfloat16).reshape(seq_rows, heads_here, HD)
    )

    def attend_back(carry, inputs):
        d_key_acc, d_value_acc = carry
        first_row, log_rows = inputs
        scores, query_blk, key_blk, value_blk, key_start = block_scores(first_row)
        attn_probs = jnp.exp(scores - log_rows[..., None])
        probs_b = attn_probs.astype(jnp.bfloat16)
        d_context_blk = lax.dynamic_slice_in_dim(d_context, first_row, q_block, 0)
        d_probs = jnp.einsum(
            "qhd,kd->hqk", d_context_blk, value_blk, preferred_element_type=jnp.float32
        )
        d_value_blk = jnp.einsum(
            "hqk,qhd->kd", probs_b, d_context_blk, preferred_element_type=jnp.float32
        )
        row_inner = jnp.sum(attn_probs * d_probs, axis=-1, keepdims=True)
        d_scores = (attn_probs * (d_probs - row_inner)).astype(jnp.bfloat16)
        d_query_blk = (
            jnp.einsum("hqk,kd->qhd", d_scores, key_blk, preferred_element_type=jnp.float32)
            * score_scale
        )
        d_key_blk = (
            jnp.einsum("hqk,qhd->kd", d_scores, query_blk, preferred_element_type=jnp.float32)
            * score_scale
        )
        d_key_acc = d_key_acc + d_key_blk
        d_value_acc = d_value_acc + d_value_blk
        return ((d_key_acc, d_value_acc), d_query_blk)

    zero_rows = jnp.zeros((seq_rows, HD), jnp.float32)
    (d_keys, d_values), d_queries = lax.scan(
        attend_back, (zero_rows, zero_rows), (starts, log_total)
    )
    d_queries = d_queries.reshape(seq_rows, heads_here, HD)

    def query_prepare(raw_rows, gain_row):
        return prepare(raw_rows, gain_row, cos_heads, sin_heads)

    def key_prepare(raw_rows, gain_row):
        return prepare(raw_rows, gain_row, cos_rows, sin_rows)

    _, query_back = jax.vjp(query_prepare, query_raw, gain_query)
    d_query_f, gain_query_part = query_back(d_queries)
    _, key_back = jax.vjp(key_prepare, key_raw, gain_key)
    d_key_f, gain_key_part = key_back(d_keys)
    d_query_b = d_query_f.reshape(seq_rows, heads_here * HD).astype(jnp.bfloat16)
    d_keyval_part = jnp.concatenate([d_key_f, d_values], axis=1)
    summed_back = lax.psum_scatter(
        jnp.concatenate([project_back(d_query_b, query_full), d_keyval_part], axis=1).astype(
            jnp.bfloat16
        ),
        "tensor",
        scatter_dimension=0,
        tiled=True,
    ).astype(jnp.float32)
    d_keyval_b = summed_back[:, model_width:].astype(jnp.bfloat16)
    d_attn_input = summed_back[:, :model_width] + project_back(d_keyval_b, keyval_full)
    query_part = contract_rows(attn_input, d_query_b)
    keyval_part = contract_rows(attn_local, d_keyval_b)
    d_in, gain_in_part = norm_back(x_local, gain_in, d_attn_input)
    grad_x = d_mid + d_in
    grad_query, grad_out = (
        lax.psum_scatter(
            query_part.astype(jnp.bfloat16), "dp", scatter_dimension=0, tiled=True
        ).astype(jnp.float32),
        lax.psum_scatter(
            out_part.astype(jnp.bfloat16), "dp", scatter_dimension=1, tiled=True
        ).astype(jnp.float32),
    )
    shared = lax.psum(
        (
            keyval_part,
            gain_in_part,
            grad_gain_post_attn,
            grad_gain_pre_ff,
            grad_gain_post_ff,
            gain_query_part,
            gain_key_part,
        ),
        ("dp", "tensor"),
    )
    shard_rows = keyval_part.shape[0] // lax.axis_size("dp")
    grad_keyval = lax.dynamic_slice_in_dim(
        shared[0], lax.axis_index("dp") * shard_rows, shard_rows, 0
    )
    return (
        output,
        grad_x,
        grad_query,
        grad_keyval,
        grad_out,
        grad_gate,
        grad_up,
        grad_down,
        shared[1],
        shared[2],
        shared[3],
        shared[4],
        shared[5],
        shared[6],
    )


def solution(mesh):
    return jax.shard_map(
        per_device,
        mesh=mesh,
        in_specs=(
            P(("dp", "tensor"), None),
            P("dp", None),
            P(("dp", "tensor"), None),
            P("dp", "tensor"),
            P("dp", None),
            P("tensor", "dp"),
            P("dp", "tensor"),
            P("dp", "tensor"),
            P("tensor", "dp"),
            P(),
            P(),
            P(),
            P(),
            P(),
            P(),
        ),
        out_specs=(
            P(("dp", "tensor"), None),
            P(("dp", "tensor"), None),
            P("dp", "tensor"),
            P("dp", None),
            P("tensor", "dp"),
            P("dp", "tensor"),
            P("dp", "tensor"),
            P("tensor", "dp"),
            P(),
            P(),
            P(),
            P(),
            P(),
            P(),
        ),
        check_vma=False,
    )
```

profile of v0, /device:TPU:3, one launch (start us, length us, event | category | flops | bytes accessed | tf_op | source)
XLA Modules:
  0.0 1214.9 jit_solution(458349446832109344)
XLA Ops:
  10.3 87.0 %all-gather.1 = bf16[32,20,512]{2,1,0:T(8,128)(2,1)S(1)} all-gather(bf16[1,20,512]{2,1,0:T(8,128)(2,1)} %bitcast.278), channel_id=1, replica_groups=mesh['dp'=32,'tensor'=4] {'dp'}, dimensions={0}, use_global_device_ids=true | all-gather | bytes 675840 | tf_op jit(solution)/shard_map/all_gather | solution.py:102
  97.5 75.5 %all-gather = bf16[32,20,256]{2,1,0:T(8,128)(2,1)S(1)} all-gather(bf16[1,20,256]{2,1,0:T(8,128)(2,1)S(1)} %bitcast.282), channel_id=1, replica_groups=mesh['dp'=32,'tensor'=4] {'dp'}, dimensions={0}, use_global_device_ids=true | all-gather | bytes 337920 | tf_op jit(solution)/shard_map/all_gather | solution.py:101
  174.8 77.2 %all-gather.2 = bf16[32,20,256]{2,1,0:T(8,128)(2,1)S(1)} all-gather(bf16[1,20,256]{2,1,0:T(8,128)(2,1)S(1)} %bitcast.283), channel_id=1, replica_groups=mesh['dp'=32,'tensor'=4] {'dp'}, dimensions={0}, use_global_device_ids=true | all-gather | bytes 337920 | tf_op jit(solution)/shard_map/all_gather | solution.py:103
  253.2 2.5 fusion.103
  259.5 5.5 fusion.60
  268.5 14.0 %while.33 = (s32[]{:T(128)}, bf16[2,512,1,256]{3,1,2,0:T(8,128)(2,1)S(1)}, f32[2,1,512]{2,1,0:T(1,128)S(1)}, s32[2]{0:T(128)S(1)}, s32[1024]{0:T(1024)S(1)}, /*i...) while((s32[]{:T(128)}, ...), condition=%wide.region_8.9_spmd.clone, body=%wide.region_5.8_spmd.sunk.clone | while | flops 544211968 | bytes 8169671 | solution.py:141
  284.7 68.5 %reduce-scatter.15.cloned.1.call-done = f32[256,640]{1,0:T(8,128)} async-done(((f32[1024,640]{1,0:T(8,128)}), f32[256,640]{1,0:T(8,128)}) %reduce-scatter.15.cloned.1.call-update) | async-done | bytes 655376 | tf_op jit(solution)/shard_map/reduce_scatter | solution.py:144
  356.9 85.5 %all-gather.3 = bf16[32,20,512]{2,1,0:T(8,128)(2,1)S(1)} all-gather(bf16[1,20,512]{2,1,0:T(8,128)(2,1)S(1)} %bitcast.279), channel_id=1, replica_groups=mesh['dp'=32,'tensor'=4] {'dp'}, dimensions={0}, use_global_device_ids=true | all-gather | bytes 675840 | tf_op jit(solution)/shard_map/all_gather | solution.py:153
  442.6 78.4 %all-gather.4 = bf16[32,20,512]{2,1,0:T(8,128)(2,1)S(1)} all-gather(bf16[1,20,512]{2,1,0:T(8,128)(2,1)S(1)} %bitcast.280), channel_id=1, replica_groups=mesh['dp'=32,'tensor'=4] {'dp'}, dimensions={0}, use_global_device_ids=true | all-gather | bytes 675840 | tf_op jit(solution)/shard_map/all_gather | solution.py:154
  521.9 80.4 %all-gather.5 = bf16[32,20,512]{2,1,0:T(8,128)(2,1)S(1)} all-gather(bf16[1,20,512]{2,1,0:T(8,128)(2,1)S(1)} %bitcast.281), channel_id=1, replica_groups=mesh['dp'=32,'tensor'=4] {'dp'}, dimensions={0}, use_global_device_ids=true | all-gather | bytes 675840 | tf_op jit(solution)/shard_map/all_gather | solution.py:155
  603.3 2.4 fusion.105
  605.8 2.6 multiply_convert_fusion.1
  609.4 2.5 fusion.106
  612.0 67.1 %reduce-scatter.17.cloned.1.call-done = f32[256,640]{1,0:T(8,128)} async-done(((f32[1024,640]{1,0:T(8,128)}), f32[256,640]{1,0:T(8,128)}) %reduce-scatter.17.cloned.1.call-update) | async-done | bytes 655376 | tf_op jit(solution)/shard_map/reduce_scatter | solution.py:162
  683.4 23.6 %all-gather.15.cloned.1.call-done = bf16[1024,640]{1,0:T(8,128)(2,1)} async-done(((bf16[256,640]{1,0:T(8,128)(2,1)}), bf16[1024,640]{1,0:T(8,128)(2,1)}) %all-gather.15.cloned.1.call-update) | async-done | bytes 1310736 | tf_op jit(solution)/shard_map/all_gather | solution.py:171
  706.9 5.2 multiply_convert_fusion
  713.7 2.5 convolution_add_fusion.1
  716.3 33.3 %reduce-scatter.19.cloned.1.call-done = f32[256,640]{1,0:T(8,128)} async-done(((f32[1024,640]{1,0:T(8,128)}), f32[256,640]{1,0:T(8,128)}) %reduce-scatter.19.cloned.1.call-update) | async-done | bytes 655376 | tf_op jit(solution)/shard_map/reduce_scatter | solution.py:180
  753.5 23.9 %all-gather.17.cloned.1.call-done = bf16[1024,640]{1,0:T(8,128)(2,1)} async-done(((bf16[256,640]{1,0:T(8,128)(2,1)}), bf16[1024,640]{1,0:T(8,128)(2,1)}) %all-gather.17.cloned.1.call-update) | async-done | bytes 1310736 | tf_op jit(solution)/shard_map/all_gather | solution.py:200
  777.4 2.8 fusion.46
  780.1 36.4 %while.34 = (s32[]{:T(128)}, f32[1024,256]{1,0:T(8,128)}, f32[1024,256]{1,0:T(8,128)}, f32[2,512,1,256]{3,1,2,0:T(8,128)}, s32[2]{0:T(128)S(1)}, /*index=5*/s32[...) while((s32[]{:T(128)}, f32[1024,256]{1,0:T(8,128)}, ...), condition=%wide.region_20.21_spmd.clone.clone, body=%wide.region_18.20_spmd.clone.sunk.clone | while | flops 1351484416 | bytes 46170532 | solution.py:234
  782.8 2.9 fusion.204
  787.1 3.0 fusion.205
  790.4 2.5 fusion.207
  795.5 2.5 convolution_add_fusion.5
  800.6 2.9 fusion.204
  805.0 3.0 fusion.205
  808.3 2.9 fusion.207
  813.7 2.9 convolution_add_fusion.5
  818.2 3.5 fusion.64
  821.8 4.1 fusion.67
  829.0 3.5 fusion.54
  832.6 4.1 multiply_reduce_fusion
  848.4 102.7 %fusion.97 = (bf16[24,256]{1,0:T(8,128)(2,1)S(1)}, bf16[256,24]{0,1:T(8,128)(2,1)S(1)}, bf16[24,512]{1,0:T(8,128)(2,1)S(1)}, bf16[24,512]{1,0:T(8,128)(2,1)S(1)}, bf16[512,24]{0,1:T(8,128)(2,1)S(1)}) fusion(bf16[640,256]{1,0:T(8,128)(2,1)S(1)} %convolution_convert_fusion.6, bf16[256,640]{0,1:T(8,128)(2,1)S(1)} %convolution_convert_fusion.5, ...), kind=kCustom, calls=%all-reduce-scatter.5 | all-reduce-scatter fusion | flops 1572865 | bytes 2720256
  953.7 5.4 collective-permute-start.17
  961.1 4.8 collective-permute-start.5
  967.2 6.1 collective-permute-start.6
  973.3 3.2 collective-permute-start.7
  976.5 2.5 collective-permute-start.8
  979.0 5.1 collective-permute-start.9
  984.1 3.2 collective-permute-start
  989.7 4.9 collective-permute-start.2
  1000.4 5.2 collective-permute-start.25
  1014.6 4.6 collective-permute-start.19
  1026.9 4.6 collective-permute-start.13
  1041.4 2.4 fusion.85
  1045.5 81.1 %all-reduce.14 = (f32[640]{0:T(1024)}, f32[640]{0:T(1024)}, f32[640]{0:T(1024)}, f32[640]{0:T(1024)}, f32[256]{0:T(256)}, /*index=5*/f32[256]{0:T(256)}) all-reduce(f32[640]{0:T(1024)S(1)} %get-tuple-element.396, f32[640]{0:T(1024)S(1)} %get-tuple-element.392, ...), channel_id=1, replica_groups=mesh['dp'=32,'tensor'=4] {'dp','tensor'}, use_global_device_ids=true, to_apply=%region_32.33 | all-reduce | flops 3072 | bytes 24576 | tf_op jit(solution)/shard_map/psum | solution.py:273
  1127.7 79.0 %all-reduce.18.cloned.1.call-done = f32[640,512]{1,0:T(8,128)} async-done(((f32[640,512]{1,0:T(8,128)}), f32[640,512]{1,0:T(8,128)}) %all-reduce.18.cloned.1.call-update) | async-done | bytes 1310736 | tf_op jit(solution)/shard_map/psum | solution.py:273
  (326 shorter events, 108.3 us)
Async XLA Ops:
  7.2 90.3 %copy-start.55 = (bf16[20,256]{1,0:T(8,128)(2,1)S(1)}, bf16[20,256]{1,0:T(8,128)(2,1)}, u32[]{:S(2)}) copy-start(bf16[20,256]{1,0:T(8,128)(2,1)} %param.22) | copy-start | bytes 30724
  7.2 246.0 %all-gather.11.cloned.1.call-start = ((), (), s32[]{:S(2)}) async-start(), calls=%async_computation.4 | async-start | bytes 1638400 | tf_op jit(solution)/shard_map/all_gather | solution.py:105
  8.4 164.7 %copy-start.45 = (s32[1,1024]{1,0:T(1,128)S(1)}, s32[1,1024]{1,0:T(1,128)}, u32[]{:S(2)}) copy-start(s32[1,1024]{1,0:T(1,128)} %param.20) | copy-start | bytes 12292
  8.4 166.4 %copy-start.56 = (bf16[256,20]{0,1:T(8,128)(2,1)S(1)}, bf16[256,20]{0,1:T(8,128)(2,1)}, u32[]{:S(2)}) copy-start(bf16[256,20]{0,1:T(8,128)(2,1)} %param.24) | copy-start | bytes 30724
  10.3 343.0 %reduce-scatter.15.cloned.1.call-start = ((), (), s32[]{:S(2)}) async-start(), calls=%async_computation.5 | async-start | bytes 3276800 | tf_op jit(solution)/shard_map/reduce_scatter | solution.py:144
  97.5 158.2 %copy-start.24 = (bf16[640,512]{1,0:T(8,128)(2,1)}, bf16[640,512]{1,0:T(8,128)(2,1)S(1)}, u32[]{:S(2)}) copy-start(bf16[640,512]{1,0:T(8,128)(2,1)S(1)} %reshape.726) | copy-start | bytes 1966084
  173.1 83.2 %copy-start.21 = (bf16[640,256]{1,0:T(8,128)(2,1)}, bf16[640,256]{1,0:T(8,128)(2,1)S(1)}, u32[]{:S(2)}) copy-start(bf16[640,256]{1,0:T(8,128)(2,1)S(1)} %reshape.724) | copy-start | bytes 983044
  284.7 318.6 %all-gather.13.cloned.1.call-start = ((), (), s32[]{:S(2)}) async-start(), calls=%async_computation.6 | async-start | bytes 1638400 | tf_op jit(solution)/shard_map/all_gather | solution.py:157
  355.9 86.7 %copy-start.49 = (bf16[20,512]{1,0:T(8,128)(2,1)S(1)}, bf16[20,512]{1,0:T(8,128)(2,1)}, u32[]{:S(2)}) copy-start(bf16[20,512]{1,0:T(8,128)(2,1)} %param.26) | copy-start | bytes 61444
  356.8 322.4 %reduce-scatter.17.cloned.1.call-start = ((), (), s32[]{:S(2)}) async-start(), calls=%async_computation.7 | async-start | bytes 3276800 | tf_op jit(solution)/shard_map/reduce_scatter | solution.py:162
  356.9 165.1 %copy-start.50 = (bf16[512,20]{0,1:T(8,128)(2,1)S(1)}, bf16[512,20]{0,1:T(8,128)(2,1)}, u32[]{:S(2)}) copy-start(bf16[512,20]{0,1:T(8,128)(2,1)} %param.27) | copy-start | bytes 61444
  612.0 94.9 %all-gather.15.cloned.1.call-start = ((), (), s32[]{:S(2)}) async-start(), calls=%async_computation.8 | async-start | bytes 1638400 | tf_op jit(solution)/shard_map/all_gather | solution.py:171
  683.0 66.6 %reduce-scatter.19.cloned.1.call-start = ((), (), s32[]{:S(2)}) async-start(), calls=%async_computation.9 | async-start | bytes 3276800 | tf_op jit(solution)/shard_map/reduce_scatter | solution.py:180
  716.3 61.1 %all-gather.17.cloned.1.call-start = ((), (), s32[]{:S(2)}) async-start(), calls=%async_computation.10 | async-start | bytes 1638400 | tf_op jit(solution)/shard_map/all_gather | solution.py:200
  753.4 288.0 %reduce-scatter.21.cloned.1.call-start = ((), (), s32[]{:S(2)}) async-start(), calls=%async_computation.11 | async-start | bytes 2949120 | tf_op jit(solution)/shard_map/reduce_scatter | solution.py:251
  840.1 366.6 %all-reduce.18.cloned.1.call-start = ((), (), s32[]{:S(2)}) async-start(), calls=%async_computation.12 | async-start | bytes 2621440 | tf_op jit(solution)/shard_map/psum | solution.py:273
  847.8 162.5 %copy-start.57 = (u32[128]{0:T(128)S(1)}, u32[128]{0:T(128)}, u32[]{:S(2)}) copy-start(u32[128]{0:T(128)} %constant.192) | copy-start | bytes 1540
  848.4 193.1 %copy-start.19 = (bf16[256,640]{1,0:T(8,128)(2,1)S(1)}, bf16[256,640]{1,0:T(8,128)(2,1)}, u32[]{:S(2)}) copy-start(bf16[256,640]{1,0:T(8,128)(2,1)} %fusion.73) | copy-start | bytes 983044
  951.1 22.2 %collective-permute-start.29 = (bf16[512,4]{0,1:T(4,128)(2,1)S(1)}, bf16[512,4]{0,1:T(4,128)(2,1)S(1)}, u32[]{:S(2)}, u32[]{:S(2)}) collective-permute-start(bf16[512,4]{0,1:T(4,128)(2,1)S(1)} %slice.73), channel_id=1, source_target_pairs={{0,24},{4,28},{8,32},{12,36},{16,40},{20,44},{24,48},{28,52},{32,5... | collective-permute-start | bytes 12296
  952.4 24.1 %collective-permute-start.23 = (bf16[4,512]{1,0:T(4,128)(2,1)S(1)}, bf16[4,512]{1,0:T(4,128)(2,1)S(1)}, u32[]{:S(2)}, u32[]{:S(2)}) collective-permute-start(bf16[4,512]{1,0:T(4,128)(2,1)S(1)} %slice.72), channel_id=1, source_target_pairs={{0,24},{4,28},{8,32},{12,36},{16,40},{20,44},{24,48},{28,52},{32,5... | collective-permute-start | bytes 12296
  953.7 25.3 %collective-permute-start.17 = (bf16[4,512]{1,0:T(4,128)(2,1)S(1)}, bf16[4,512]{1,0:T(4,128)(2,1)S(1)}, u32[]{:S(2)}, u32[]{:S(2)}) collective-permute-start(bf16[4,512]{1,0:T(4,128)(2,1)S(1)} %slice.71), channel_id=1, source_target_pairs={{0,24},{4,28},{8,32},{12,36},{16,40},{20,44},{24,48},{28,52},{32,5... | collective-permute-start | bytes 12296
  959.1 6.7 collective-permute-start.11
  961.1 6.1 collective-permute-start.5
  965.9 18.2 %collective-permute-start.10 = (bf16[256,24]{0,1:T(8,128)(2,1)S(1)}, bf16[256,24]{0,1:T(8,128)(2,1)S(1)}, u32[]{:S(2)}, u32[]{:S(2)}) collective-permute-start(bf16[256,24]{0,1:T(8,128)(2,1)S(1)} %get-tuple-element.452), channel_id=1, source_target_pairs={{0,20},{4,24},{8,28},{12,32},{16,36},{20,40},{24,44},{28,48},{32,5... | collective-permute-start | bytes 36872
  967.2 20.1 %collective-permute-start.6 = (bf16[256,24]{0,1:T(8,128)(2,1)S(1)}, bf16[256,24]{0,1:T(8,128)(2,1)S(1)}, u32[]{:S(2)}, u32[]{:S(2)}) collective-permute-start(bf16[256,24]{0,1:T(8,128)(2,1)S(1)} %get-tuple-element.452), channel_id=1, source_target_pairs={{0,4},{4,8},{8,12},{12,16},{16,20},{20,24},{24,28},{28,32},{32,36}... | collective-permute-start | bytes 36872
  973.3 16.4 %collective-permute-start.7 = (bf16[256,24]{0,1:T(8,128)(2,1)S(1)}, bf16[256,24]{0,1:T(8,128)(2,1)S(1)}, u32[]{:S(2)}, u32[]{:S(2)}) collective-permute-start(bf16[256,24]{0,1:T(8,128)(2,1)S(1)} %get-tuple-element.452), channel_id=1, source_target_pairs={{0,8},{4,12},{8,16},{12,20},{16,24},{20,28},{24,32},{28,36},{32,40... | collective-permute-start | bytes 36872
  976.5 18.2 %collective-permute-start.8 = (bf16[256,24]{0,1:T(8,128)(2,1)S(1)}, bf16[256,24]{0,1:T(8,128)(2,1)S(1)}, u32[]{:S(2)}, u32[]{:S(2)}) collective-permute-start(bf16[256,24]{0,1:T(8,128)(2,1)S(1)} %get-tuple-element.452), channel_id=1, source_target_pairs={{0,12},{4,16},{8,20},{12,24},{16,28},{20,32},{24,36},{28,40},{32,4... | collective-permute-start | bytes 36872
  979.0 17.6 %collective-permute-start.9 = (bf16[256,24]{0,1:T(8,128)(2,1)S(1)}, bf16[256,24]{0,1:T(8,128)(2,1)S(1)}, u32[]{:S(2)}, u32[]{:S(2)}) collective-permute-start(bf16[256,24]{0,1:T(8,128)(2,1)S(1)} %get-tuple-element.452), channel_id=1, source_target_pairs={{0,16},{4,20},{8,24},{12,28},{16,32},{20,36},{24,40},{28,44},{32,4... | collective-permute-start | bytes 36872
  984.1 14.7 %collective-permute-start = (bf16[24,256]{1,0:T(8,128)(2,1)S(1)}, bf16[24,256]{1,0:T(8,128)(2,1)S(1)}, u32[]{:S(2)}, u32[]{:S(2)}) collective-permute-start(bf16[24,256]{1,0:T(8,128)(2,1)S(1)} %get-tuple-element.451), channel_id=1, source_target_pairs={{0,4},{4,8},{8,12},{12,16},{16,20},{20,24},{24,28},{28,32},{32,36}... | collective-permute-start | bytes 36872
  987.3 13.1 %collective-permute-start.1 = (bf16[24,256]{1,0:T(8,128)(2,1)S(1)}, bf16[24,256]{1,0:T(8,128)(2,1)S(1)}, u32[]{:S(2)}, u32[]{:S(2)}) collective-permute-start(bf16[24,256]{1,0:T(8,128)(2,1)S(1)} %get-tuple-element.451), channel_id=1, source_target_pairs={{0,8},{4,12},{8,16},{12,20},{16,24},{20,28},{24,32},{28,36},{32,40... | collective-permute-start | bytes 36872
  989.7 16.0 %collective-permute-start.2 = (bf16[24,256]{1,0:T(8,128)(2,1)S(1)}, bf16[24,256]{1,0:T(8,128)(2,1)S(1)}, u32[]{:S(2)}, u32[]{:S(2)}) collective-permute-start(bf16[24,256]{1,0:T(8,128)(2,1)S(1)} %get-tuple-element.451), channel_id=1, source_target_pairs={{0,12},{4,16},{8,20},{12,24},{16,28},{20,32},{24,36},{28,40},{32,4... | collective-permute-start | bytes 36872
  994.6 12.4 %collective-permute-start.3 = (bf16[24,256]{1,0:T(8,128)(2,1)S(1)}, bf16[24,256]{1,0:T(8,128)(2,1)S(1)}, u32[]{:S(2)}, u32[]{:S(2)}) collective-permute-start(bf16[24,256]{1,0:T(8,128)(2,1)S(1)} %get-tuple-element.451), channel_id=1, source_target_pairs={{0,16},{4,20},{8,24},{12,28},{16,32},{20,36},{24,40},{28,44},{32,4... | collective-permute-start | bytes 36872
  996.6 12.0 collective-permute-start.4
  998.8 13.6 %collective-permute-start.24 = (bf16[512,24]{0,1:T(8,128)(2,1)S(1)}, bf16[512,24]{0,1:T(8,128)(2,1)S(1)}, u32[]{:S(2)}, u32[]{:S(2)}) collective-permute-start(bf16[512,24]{0,1:T(8,128)(2,1)S(1)} %get-tuple-element.455), channel_id=1, source_target_pairs={{0,4},{4,8},{8,12},{12,16},{16,20},{20,24},{24,28},{28,32},{32,36}... | collective-permute-start | bytes 73736
  1000.4 14.2 %collective-permute-start.25 = (bf16[512,24]{0,1:T(8,128)(2,1)S(1)}, bf16[512,24]{0,1:T(8,128)(2,1)S(1)}, u32[]{:S(2)}, u32[]{:S(2)}) collective-permute-start(bf16[512,24]{0,1:T(8,128)(2,1)S(1)} %get-tuple-element.455), channel_id=1, source_target_pairs={{0,8},{4,12},{8,16},{12,20},{16,24},{20,28},{24,32},{28,36},{32,40... | collective-permute-start | bytes 73736
  1005.7 13.6 %collective-permute-start.26 = (bf16[512,24]{0,1:T(8,128)(2,1)S(1)}, bf16[512,24]{0,1:T(8,128)(2,1)S(1)}, u32[]{:S(2)}, u32[]{:S(2)}) collective-permute-start(bf16[512,24]{0,1:T(8,128)(2,1)S(1)} %get-tuple-element.455), channel_id=1, source_target_pairs={{0,12},{4,16},{8,20},{12,24},{16,28},{20,32},{24,36},{28,40},{32,4... | collective-permute-start | bytes 73736
  1007.0 13.8 %collective-permute-start.27 = (bf16[512,24]{0,1:T(8,128)(2,1)S(1)}, bf16[512,24]{0,1:T(8,128)(2,1)S(1)}, u32[]{:S(2)}, u32[]{:S(2)}) collective-permute-start(bf16[512,24]{0,1:T(8,128)(2,1)S(1)} %get-tuple-element.455), channel_id=1, source_target_pairs={{0,16},{4,20},{8,24},{12,28},{16,32},{20,36},{24,40},{28,44},{32,4... | collective-permute-start | bytes 73736
  1008.6 13.5 %collective-permute-start.28 = (bf16[512,24]{0,1:T(8,128)(2,1)S(1)}, bf16[512,24]{0,1:T(8,128)(2,1)S(1)}, u32[]{:S(2)}, u32[]{:S(2)}) collective-permute-start(bf16[512,24]{0,1:T(8,128)(2,1)S(1)} %get-tuple-element.455), channel_id=1, source_target_pairs={{0,20},{4,24},{8,28},{12,32},{16,36},{20,40},{24,44},{28,48},{32,5... | collective-permute-start | bytes 73736
  1012.4 12.9 %collective-permute-start.18 = (bf16[24,512]{1,0:T(8,128)(2,1)S(1)}, bf16[24,512]{1,0:T(8,128)(2,1)S(1)}, u32[]{:S(2)}, u32[]{:S(2)}) collective-permute-start(bf16[24,512]{1,0:T(8,128)(2,1)S(1)} %get-tuple-element.454), channel_id=1, source_target_pairs={{0,4},{4,8},{8,12},{12,16},{16,20},{20,24},{24,28},{28,32},{32,36}... | collective-permute-start | bytes 73736
  1014.6 12.3 %collective-permute-start.19 = (bf16[24,512]{1,0:T(8,128)(2,1)S(1)}, bf16[24,512]{1,0:T(8,128)(2,1)S(1)}, u32[]{:S(2)}, u32[]{:S(2)}) collective-permute-start(bf16[24,512]{1,0:T(8,128)(2,1)S(1)} %get-tuple-element.454), channel_id=1, source_target_pairs={{0,8},{4,12},{8,16},{12,20},{16,24},{20,28},{24,32},{28,36},{32,40... | collective-permute-start | bytes 73736
  1019.2 12.3 %collective-permute-start.20 = (bf16[24,512]{1,0:T(8,128)(2,1)S(1)}, bf16[24,512]{1,0:T(8,128)(2,1)S(1)}, u32[]{:S(2)}, u32[]{:S(2)}) collective-permute-start(bf16[24,512]{1,0:T(8,128)(2,1)S(1)} %get-tuple-element.454), channel_id=1, source_target_pairs={{0,12},{4,16},{8,20},{12,24},{16,28},{20,32},{24,36},{28,40},{32,4... | collective-permute-start | bytes 73736
  1020.9 12.6 %collective-permute-start.21 = (bf16[24,512]{1,0:T(8,128)(2,1)S(1)}, bf16[24,512]{1,0:T(8,128)(2,1)S(1)}, u32[]{:S(2)}, u32[]{:S(2)}) collective-permute-start(bf16[24,512]{1,0:T(8,128)(2,1)S(1)} %get-tuple-element.454), channel_id=1, source_target_pairs={{0,16},{4,20},{8,24},{12,28},{16,32},{20,36},{24,40},{28,44},{32,4... | collective-permute-start | bytes 73736
  1022.2 12.6 %collective-permute-start.22 = (bf16[24,512]{1,0:T(8,128)(2,1)S(1)}, bf16[24,512]{1,0:T(8,128)(2,1)S(1)}, u32[]{:S(2)}, u32[]{:S(2)}) collective-permute-start(bf16[24,512]{1,0:T(8,128)(2,1)S(1)} %get-tuple-element.454), channel_id=1, source_target_pairs={{0,20},{4,24},{8,28},{12,32},{16,36},{20,40},{24,44},{28,48},{32,5... | collective-permute-start | bytes 73736
  1025.3 13.3 %collective-permute-start.12 = (bf16[24,512]{1,0:T(8,128)(2,1)S(1)}, bf16[24,512]{1,0:T(8,128)(2,1)S(1)}, u32[]{:S(2)}, u32[]{:S(2)}) collective-permute-start(bf16[24,512]{1,0:T(8,128)(2,1)S(1)} %get-tuple-element.453), channel_id=1, source_target_pairs={{0,4},{4,8},{8,12},{12,16},{16,20},{20,24},{24,28},{28,32},{32,36}... | collective-permute-start | bytes 73736
  1026.9 11.7 collective-permute-start.13
  1031.5 7.1 collective-permute-start.14
  1033.5 5.1 collective-permute-start.15
  1034.8 3.8 collective-permute-start.16
  (58 other events, 751.8 us)
Sparse Core Ops, SparseCore 0:
  10.4 25.2 all-gather.10
  284.8 68.4 reduce-scatter.14
  356.9 24.9 all-gather.12
  612.1 67.0 reduce-scatter.16
  683.1 23.7 all-gather.14
  716.4 33.1 reduce-scatter.18
  753.5 23.8 all-gather.16
  840.2 35.4 reduce-scatter.20
  1044.0 162.7 all-reduce.17
where the time goes:
time: 1230 us; the launch traced here: 1210 us
  blocking collectives  668 us (54%)
  waiting for transfers between devices  296 us (24%)
  starting transfers between devices  81.9 us (7%)
  matrix products  65.9 us (5%)
  other arithmetic  48.6 us (4%)
  local copies, waits for them, and re-layouts  27.5 us (2%)
  between operations  16.8 us (1%)
    unnamed x1, blocking collectives  103 us
    all_gather x1, blocking collectives, per_device(): lax.all_gather(w_keyval, 'dp', axis=0, tiled=True)  87 us
    all_gather x1, blocking collectives, per_device(): lax.all_gather(w_gate, 'dp', axis=0, tiled=True)  85.5 us
    psum x1, blocking collectives, per_device(): lax.psum((keyval_part, gain_in_part, grad_gain_post_attn, grad_gain_pre_f...  81.1 us
    unnamed x30, starting transfers between devices  81 us
    all_gather x1, blocking collectives, per_device(): lax.all_gather(w_down, 'dp', axis=1, tiled=True)  80.4 us
    psum x1, waiting for transfers between devices, per_device(): lax.psum((keyval_part, gain_in_part, grad_gain_post_attn, grad_gain_pre_f...  79 us
    all_gather x1, blocking collectives, per_device(): lax.all_gather(w_up, 'dp', axis=0, tiled=True)  78.4 us
  transfers between devices with their start and end apart: 39, of which 6 were waited for; matrix products, arithmetic and copies ran while one was open for 10% of the time, Pallas kernels for 0%

commit v1 on v0

v1 whole, which is shorter than its diff:
```python
import jax
import jax.numpy as jnp
from jax import lax
from jax.experimental import pallas as pl
from jax.experimental.pallas import tpu as pltpu
from jax.sharding import PartitionSpec as P

HD = 256
WINDOW = 512
D = 640
PART = 256
KEYS = 768
BLOCK = 352
CB = 16
GROUPS = 8
KV0, G0, U0, D0 = 80, 112, 192, 272
LANES = ((0, 112, "xyz"), (112, 128, "yzx"), (240, 112, "zxy"))
norm_eps = 1e-06
rope_base = 10000.0
MESH = pl.DeviceIdType.MESH
f32 = jnp.float32
bf16 = jnp.bfloat16


def place():
    dp = lax.axis_index("dp")
    t = lax.axis_index("tensor")
    return {
        "x": (dp // 16) * 2 + t // 2,
        "y": dp % 4,
        "z": (dp // 4) % 4,
        "c": t % 2,
    }


def device_of(p):
    return {
        "dp": (p["x"] // 2) * 16 + p["z"] * 4 + p["y"],
        "tensor": (p["x"] % 2) * 2 + p["c"],
    }


def moved(p, axis, by):
    size = 2 if axis == "c" else 4
    q = dict(p)
    q[axis] = (p[axis] + by) % size
    return q


def diagonal(p):
    q = moved(p, "c", 1)
    q["x"] = (p["x"] // 2) * 2 + (1 - p["x"] % 2)
    return q


def peers_of(p):
    found = [
        moved(p, axis, by)
        for axis, by in (("x", 1), ("x", 3), ("y", 1), ("y", 2), ("y", 3), ("z", 1), ("z", 3), ("c", 1))
    ]
    return found + [diagonal(p)]


def greet(p):
    barrier = pltpu.get_barrier_semaphore()
    peers = peers_of(p)
    for q in peers:
        pl.semaphore_signal(barrier, inc=1, device_id=device_of(q), device_id_type=MESH)
    pl.semaphore_wait(barrier, len(peers))


def send(src, dst, send_sem, recv_sem, q):
    copy = pltpu.make_async_remote_copy(
        src_ref=src,
        dst_ref=dst,
        send_sem=send_sem,
        recv_sem=recv_sem,
        device_id=device_of(q),
        device_id_type=MESH,
    )
    copy.start()
    return copy


def slab(ref, p, axis, value, gathered, first, rows, core=None):
    at = {a: (value if a == axis else p[a]) for a in "xyz"}
    every = slice(None)
    x_lo = every if "x" in gathered else at["x"] % 2
    x_hi = every if "x" in gathered else at["x"] // 2
    y = every if "y" in gathered else at["y"]
    z = every if "z" in gathered else at["z"]
    where = (x_lo,) + (() if core is None else (core,)) + (y, x_hi, z, pl.ds(first, rows), every)
    return ref.at[where]


def halves(first, rows):
    top = 64
    return ((first, top), (first + top, rows - top))


def gather_kernel(
    s_ref, x_ref, w_ref, xg_ref, got, stage, block,
    one_send, one_recv, ring_send, ring_recv, sib_send, sib_recv, x_send, x_recv, local,
):
    p = place()
    t = lax.axis_index("tensor")
    y = p["y"]
    core = p["c"]
    sibling = moved(p, "c", 1)
    dp = lax.axis_index("dp")
    greet(p)

    first = []
    for k in (1, 3, 2):
        q = moved(p, "y", k)
        first.append(send(s_ref.at[q["y"]], got.at[y], one_send.at[k - 1], one_recv.at[k - 1], q))

    def token_copy(k):
        return pltpu.make_async_remote_copy(
            src_ref=x_ref,
            dst_ref=xg_ref.at[2 - k],
            send_sem=x_send.at[k - 1],
            recv_sem=x_recv.at[k - 1],
            device_id={"dp": dp, "tensor": jnp.minimum(t + k, 3)},
            device_id_type=MESH,
        )

    for k in (1, 2):
        @pl.when(t + k <= 3)
        def _(k=k):
            token_copy(k).start()

    own_tokens = pltpu.make_async_copy(x_ref, xg_ref.at[2], local.at[0])
    own_tokens.start()

    got[pl.ds(y, 1)] = s_ref[pl.ds(y, 1)]
    for copy in first:
        copy.wait_recv()
    for j in range(4):
        stage[20 * j : 20 * j + 20, :] = got[j].astype(f32)[:20, :512]
    for i, at in enumerate((0, G0, U0, D0)):
        block[at : at + 80, :] = stage[:, 128 * i : 128 * i + 128].astype(bf16)
    block[KV0 : KV0 + 32, :] = got[pl.ds(t, 1)][0, :, 512:640]
    own_block = pltpu.make_async_copy(
        block, w_ref.at[p["x"] % 2, core, y, p["x"] // 2, p["z"]], local.at[1]
    )
    own_block.start()

    pending = list(first)
    for phase in range(3):
        started = []
        for lane, (at, rows, order) in enumerate(LANES):
            axis, gathered = order[phase], order[:phase]
            m = p[axis]
            mine = slab(w_ref, p, axis, m, gathered, at, rows, core)
            src = block.at[pl.ds(at, rows), :] if phase == 0 else mine
            up, down = moved(p, axis, 1), moved(p, axis, 3)
            sems = ring_send.at[lane, phase], ring_recv.at[lane, phase]
            to_up = send(src, mine, sems[0].at[0], sems[1].at[0], up)
            to_down = send(src, mine, sems[0].at[1], sems[1].at[1], down)
            if phase == 2:
                pending.append(send(mine, mine, sib_send.at[lane, 0], sib_recv.at[lane, 0], sibling))
            started.append((to_up, to_down, up, down, gathered, sems))
        passed = []
        for lane, (at, rows, order) in enumerate(LANES):
            axis = order[phase]
            to_up, to_down, up, down, gathered, sems = started[lane]
            low, high = halves(at, rows)
            to_up.wait_recv()
            from_down = slab(w_ref, p, axis, down[axis], gathered, *low, core)
            passed.append(send(from_down, from_down, sems[0].at[2], sems[1].at[2], up))
            to_down.wait_recv()
            from_up = slab(w_ref, p, axis, up[axis], gathered, *high, core)
            passed.append(send(from_up, from_up, sems[0].at[3], sems[1].at[3], down))
            if phase == 2:
                for i, q in ((1, down), (2, up)):
                    whole = slab(w_ref, p, axis, q[axis], gathered, at, rows, core)
                    pending.append(send(whole, whole, sib_send.at[lane, i], sib_recv.at[lane, i], sibling))
            pending += [to_up, to_down]
        for lane, (at, rows, order) in enumerate(LANES):
            axis = order[phase]
            gathered = order[:phase]
            far = (p[axis] + 2) % 4
            for i in range(2):
                passed[2 * lane + i].wait_recv()
                if phase == 2:
                    part = slab(w_ref, p, axis, far, gathered, *halves(at, rows)[i], core)
                    pending.append(send(part, part, sib_send.at[lane, 3 + i], sib_recv.at[lane, 3 + i], sibling))
        pending += passed
        if phase == 0:
            own_block.wait()
    for copy in pending:
        copy.wait_send()
    for lane in range(3):
        for i in range(5):
            at, rows, order = LANES[lane]
            axis, gathered = order[2], order[:2]
            if i < 3:
                value = (p[axis] + (0, 3, 1)[i]) % 4
                part = slab(w_ref, p, axis, value, gathered, at, rows, sibling["c"])
            else:
                value = (p[axis] + 2) % 4
                part = slab(w_ref, p, axis, value, gathered, *halves(at, rows)[i - 3], sibling["c"])
            pltpu.make_async_remote_copy(
                src_ref=part, dst_ref=part, send_sem=sib_send.at[lane, i], recv_sem=sib_recv.at[lane, i],
                device_id=device_of(sibling), device_id_type=MESH,
            ).wait_recv()
    own_tokens.wait()
    for k in (1, 2):
        @pl.when(t + k <= 3)
        def _(k=k):
            token_copy(k).wait_send()

        @pl.when(t - k >= 0)
        def _(k=k):
            token_copy(k).wait_recv()


def gather(s_rows, tokens):
    dma = pltpu.SemaphoreType.DMA
    return pl.pallas_call(
        gather_kernel,
        out_shape=(
            jax.ShapeDtypeStruct((2, 2, 4, 2, 4, BLOCK, 128), bf16),
            jax.ShapeDtypeStruct((3, PART, D), bf16),
        ),
        in_specs=[pl.BlockSpec(memory_space=pltpu.VMEM)] * 2,
        out_specs=(pl.BlockSpec(memory_space=pl.ANY), pl.BlockSpec(memory_space=pl.ANY)),
        scratch_shapes=[
            pltpu.VMEM((4, 32, D), bf16),
            pltpu.VMEM((80, 512), f32),
            pltpu.VMEM((BLOCK, 128), bf16),
            dma((3,)), dma((3,)), dma((3, 3, 4)), dma((3, 3, 4)), dma((3, 5)), dma((3, 5)),
            dma((2,)), dma((2,)), dma((2,)),
        ],
        compiler_params=pltpu.CompilerParams(
            collective_id=0, has_side_effects=True, vmem_limit_bytes=32 << 20
        ),
        name="gather_weights",
    )(s_rows, tokens)


def dot(a, b):
    return jnp.dot(a, b, preferred_element_type=f32)


def dot_nt(a, b):
    return lax.dot_general(a, b, (((1,), (1,)), ((), ())), preferred_element_type=f32)


def inv_rms(v):
    return lax.rsqrt(jnp.mean(v * v, axis=-1, keepdims=True) + norm_eps)


def norm_back(v, r, c, e):
    ec = e * c
    vr = v * r
    dv = r * (ec - vr * jnp.mean(vr * ec, axis=-1, keepdims=True))
    return dv, jnp.sum(e * vr, axis=0, keepdims=True)


def turn(u, cos, sin):
    a, b = u[:, :128], u[:, 128:]
    return jnp.concatenate([a * cos - b * sin, b * cos + a * sin], axis=1)


def turn_back(e, cos, sin):
    a, b = e[:, :128], e[:, 128:]
    return jnp.concatenate([a * cos + b * sin, b * cos - a * sin], axis=1)


def columns(w_ref, cb, first):
    return jnp.concatenate(
        [w_ref[cb + i, :, first : first + 80, :].reshape(D, 128) for i in range(2)], axis=1
    )


def put_columns(g_ref, cb, first, value):
    value = value.astype(bf16)
    for i in range(2):
        g_ref[cb + i, :, first : first + 80, :] = value[:, 128 * i : 128 * i + 128].reshape(GROUPS, 80, 128)


def layer_kernel(
    t_ref, x_ref, cot_ref, low_ref, cos_ref, sin_ref, gains_ref, head_gains_ref, w_ref,
    out_ref, gx_ref, dx_ref, g_ref, gn_ref,
    kv32, wkv, attn_in, attn_in_t, kt, vt, kb, vb, qraw, qb, probs, ctx, mlp_in, mlp_in_t, act_s, dact_s, hid_s,
    acc, acc2, dkt, dvt, dkv, mid_s, proj_s,
):
    scale = HD ** -0.5
    t = t_ref[0]
    gin, gpa, gpf, gpo = (gains_ref[i : i + 1, :] for i in range(4))
    gq, gk = head_gains_ref[0:1, :], head_gains_ref[1:2, :]
    row = lax.broadcasted_iota(jnp.int32, (KEYS, 1), 0)

    for tt in range(4):
        for yy in range(4):
            for g in range(GROUPS):
                at = 20 * (4 * g + tt)
                kv32[at : at + 20, 128 * yy : 128 * yy + 128] = (
                    w_ref[4 * tt + yy, g, KV0 : KV0 + 32, :].astype(f32)[:20]
                )
    wkv[...] = kv32[:D, :].astype(bf16)

    def tokens():
        x = x_ref[...].reshape(KEYS, D).astype(f32)
        return jnp.where(row >= (2 - t) * PART, x, 0.0)

    x = tokens()
    a = x * inv_rms(x) * gin
    attn_in[...] = a.astype(bf16)
    attn_in_t[...] = a.T.astype(bf16)

    kv_raw = dot(attn_in[...], wkv[...])
    kraw = kv_raw[:, :HD]
    dkv[...] = kraw
    k = turn(kraw * inv_rms(kraw) * gk, cos_ref[...], sin_ref[...])
    kb[...] = k.astype(bf16)
    kt[...] = k.T.astype(bf16)
    v = kv_raw[:, HD:]
    vb[...] = v.astype(bf16)
    vt[...] = v.T.astype(bf16)

    cos_q, sin_q = cos_ref[2 * PART :, :], sin_ref[2 * PART :, :]
    column = lax.broadcasted_iota(jnp.int32, (PART, KEYS), 1)
    own = lax.broadcasted_iota(jnp.int32, (PART, KEYS), 0)
    acc[...] = jnp.zeros_like(acc)

    def head(h, _):
        raw = dot(attn_in[2 * PART :, :], columns(w_ref, 4 * h, 0))
        qraw[h] = raw
        q = turn(raw * inv_rms(raw) * gq, cos_q, sin_q).astype(bf16)
        qb[h] = q
        s = dot(q, kt[...]) * scale
        s = jnp.where((column >= low_ref[...]) & (column <= own + 2 * PART), s, -1e30)
        e = jnp.exp(s - jnp.max(s, axis=-1, keepdims=True))
        pr = e / jnp.sum(e, axis=-1, keepdims=True)
        probs[h] = pr
        c = dot(pr.astype(bf16), vb[...]).astype(bf16)
        ctx[h] = c
        acc[...] += dot_nt(c, columns(w_ref, 4 * h + 2, 0))
        return 0

    lax.fori_loop(0, 4, head, 0)
    proj = acc[...]
    proj_s[...] = proj
    xf = x_ref[2].astype(f32)
    mid = xf + proj * inv_rms(proj) * gpa
    mid_s[...] = mid
    m = mid * inv_rms(mid) * gpf
    mlp_in[...] = m.astype(bf16)
    mlp_in_t[...] = m.T.astype(bf16)
    acc[...] = jnp.zeros_like(acc)

    def feed(c, _):
        gate = dot(mlp_in[...], columns(w_ref, 2 * c, G0))
        up = dot(mlp_in[...], columns(w_ref, 2 * c, U0))
        k0, k1 = 0.7978845608028654, 0.044715
        sq = gate * gate
        th = jnp.tanh(k0 * (gate + k1 * gate * sq))
        half = 0.5 * (1.0 + th)
        act = gate * half
        hid = (act * up).astype(bf16)
        act_s[c] = act
        dact_s[c] = up * (half + 0.5 * gate * (1.0 - th * th) * (k0 + (3.0 * k0 * k1) * sq))
        hid_s[c] = hid
        acc[...] += dot_nt(hid, columns(w_ref, 2 * c, D0))
        return 0

    lax.fori_loop(0, 8, feed, 0)
    mlp = acc[...]
    r = inv_rms(mlp)
    out_ref[...] = (mid_s[...] + mlp * r * gpo).astype(bf16)
    top = cot_ref[...].astype(f32)
    d_mlp, g_po = norm_back(mlp, r, gpo, top)
    gn_ref[3:4, :] = g_po
    d_mlp_b = d_mlp.astype(bf16)
    d_mlp_t = d_mlp.T.astype(bf16)
    ctx_in = d_mlp_b
    acc[...] = jnp.zeros_like(acc)

    def feed_back(c, _):
        put_columns(g_ref, 2 * c, D0, dot(d_mlp_t, hid_s[c]))
        d_hid = dot(ctx_in, columns(w_ref, 2 * c, D0))
        d_gate = (d_hid * dact_s[c]).astype(bf16)
        d_up = (d_hid * act_s[c]).astype(bf16)
        put_columns(g_ref, 2 * c, G0, dot(mlp_in_t[...], d_gate))
        put_columns(g_ref, 2 * c, U0, dot(mlp_in_t[...], d_up))
        acc[...] += dot_nt(d_gate, columns(w_ref, 2 * c, G0)) + dot_nt(d_up, columns(w_ref, 2 * c, U0))
        return 0

    lax.fori_loop(0, 8, feed_back, 0)
    mid = mid_s[...]
    d_pre, g_pf = norm_back(mid, inv_rms(mid), gpf, acc[...])
    gn_ref[2:3, :] = g_pf
    d_mid = cot_ref[...].astype(f32) + d_pre
    proj = proj_s[...]
    d_proj, g_pa = norm_back(proj, inv_rms(proj), gpa, d_mid)
    gn_ref[1:2, :] = g_pa
    gx_ref[...] = d_mid
    d_proj_b = d_proj.astype(bf16)
    d_proj_t = d_proj.T.astype(bf16)
    dkt[...] = jnp.zeros_like(dkt)
    dvt[...] = jnp.zeros_like(dvt)
    acc[...] = jnp.zeros_like(acc)
    acc2[...] = jnp.zeros_like(acc2)

    def head_back(h, _):
        put_columns(g_ref, 4 * h + 2, 0, dot(d_proj_t, ctx[h]))
        d_ctx = dot(d_proj_b, columns(w_ref, 4 * h + 2, 0))
        d_ctx_b = d_ctx.astype(bf16)
        pr = probs[h]
        d_pr = dot(d_ctx_b, vt[...])
        dvt[...] += dot(d_ctx.T.astype(bf16), pr.astype(bf16))
        inner = jnp.sum(pr * d_pr, axis=-1, keepdims=True)
        ds = (pr * (d_pr - inner)).astype(bf16)
        dq = dot(ds, kb[...]) * scale
        dkt[...] += dot(qb[h].astype(f32).T.astype(bf16), ds)
        raw = qraw[h]
        d_raw, g_q = norm_back(raw, inv_rms(raw), gq, turn_back(dq, cos_q, sin_q))
        acc2[...] += g_q
        d_raw = d_raw.astype(bf16)
        put_columns(g_ref, 4 * h, 0, dot(attn_in_t[:, 2 * PART :], d_raw))
        acc[...] += dot_nt(d_raw, columns(w_ref, 4 * h, 0))
        return 0

    lax.fori_loop(0, 4, head_back, 0)
    gn_ref[4:8, :] = jnp.zeros((4, D), f32)
    gn_ref[4:5, :HD] = acc2[...]
    raw = dkv[...]
    dk, g_k = norm_back(raw, inv_rms(raw), gk, turn_back(dkt[...].T * scale, cos_ref[...], sin_ref[...]))
    gn_ref[5:6, :HD] = g_k
    d_kv = jnp.concatenate([dk, dvt[...].T], axis=1).astype(bf16)
    kv32[:D, :] = dot(attn_in_t[...], d_kv)
    kv32[D:, :] = jnp.zeros((16, 512), f32)
    for tt in range(4):
        for yy in range(4):
            for g in range(GROUPS):
                at = 20 * (4 * g + tt)
                g_ref[4 * tt + yy, g, KV0 : KV0 + 32, :] = (
                    kv32[at : at + 32, 128 * yy : 128 * yy + 128].astype(bf16)
                )
    d_in = dot_nt(d_kv, wkv[...])
    d_in = jnp.concatenate([d_in[: 2 * PART], d_in[2 * PART :] + acc[...]], axis=0)
    x = tokens()
    dx, g_in = norm_back(x, inv_rms(x), gin, d_in)
    gn_ref[0:1, :] = g_in
    gx_ref[...] += dx[2 * PART :]
    dx_ref[...] = dx[: 2 * PART].reshape(2, PART, D).astype(bf16)


def layer(t, x_parts, cotangent, low, cos, sin, gains, head_gains, weights):
    vmem = pl.BlockSpec(memory_space=pltpu.VMEM)
    return pl.pallas_call(
        layer_kernel,
        out_shape=(
            jax.ShapeDtypeStruct((PART, D), bf16),
            jax.ShapeDtypeStruct((PART, D), f32),
            jax.ShapeDtypeStruct((2, PART, D), bf16),
            jax.ShapeDtypeStruct((CB, GROUPS, BLOCK, 128), bf16),
            jax.ShapeDtypeStruct((8, D), f32),
        ),
        in_specs=[pl.BlockSpec(memory_space=pltpu.SMEM)] + [vmem] * 8,
        out_specs=(vmem,) * 5,
        scratch_shapes=[
            pltpu.VMEM((D + 16, 512), f32),
            pltpu.VMEM((D, 512), bf16),
            pltpu.VMEM((KEYS, D), bf16),
            pltpu.VMEM((D, KEYS), bf16),
            pltpu.VMEM((HD, KEYS), bf16),
            pltpu.VMEM((HD, KEYS), bf16),
            pltpu.VMEM((KEYS, HD), bf16),
            pltpu.VMEM((KEYS, HD), bf16),
            pltpu.VMEM((4, PART, HD), f32),
            pltpu.VMEM((4, PART, HD), bf16),
            pltpu.VMEM((4, PART, KEYS), f32),
            pltpu.VMEM((4, PART, HD), bf16),
            pltpu.VMEM((PART, D), bf16),
            pltpu.VMEM((D, PART), bf16),
            pltpu.VMEM((8, PART, 256), f32),
            pltpu.VMEM((8, PART, 256), f32),
            pltpu.VMEM((8, PART, 256), bf16),
            pltpu.VMEM((PART, D), f32),
            pltpu.VMEM((1, HD), f32),
            pltpu.VMEM((HD, KEYS), f32),
            pltpu.VMEM((HD, KEYS), f32),
            pltpu.VMEM((KEYS, HD), f32),
            pltpu.VMEM((PART, D), f32),
            pltpu.VMEM((PART, D), f32),
        ],
        compiler_params=pltpu.CompilerParams(vmem_limit_bytes=60 << 20),
        name="layer",
    )(t, x_parts, cotangent, low, cos, sin, gains, head_gains, weights)


def slab_shape(gathered, rows):
    x = (2,) if "x" in gathered else ()
    y = (4,) if "y" in gathered else ()
    z = (4,) if "z" in gathered else ()
    return x + y + x + z + (rows, 128)


def add_blocks(acc, p, axis, value, gathered, first, rows, terms):
    sizes = slab_shape(gathered, rows)[:-2]
    count = 1
    for n in sizes:
        count *= n

    def step(i, _):
        index = []
        rest = i
        for n in reversed(sizes):
            index.append(rest % n)
            rest = rest // n
        index = index[::-1]
        at = iter(index)
        x_lo = next(at) if "x" in gathered else (value if axis == "x" else p["x"]) % 2
        y = next(at) if "y" in gathered else (value if axis == "y" else p["y"])
        x_hi = next(at) if "x" in gathered else (value if axis == "x" else p["x"]) // 2
        z = next(at) if "z" in gathered else (value if axis == "z" else p["z"])
        target = (x_lo, y, x_hi, z, pl.ds(first, rows), slice(None))
        total = acc[target].astype(f32)
        for term in terms:
            total = total + term[tuple(index)].astype(f32)
        acc[target] = total.astype(bf16)
        return 0

    if count == 1:
        step(0, 0)
    else:
        lax.fori_loop(0, count, step, 0)


def reduce_kernel(
    g_ref, dx_ref, gx_ref, gn_ref, shard_ref, kv_ref, gx_out, gn_out,
    acc, other, *rest,
):
    bufs, rest = rest[:27], rest[27:]
    (
        dx_got, gn_now, gn_got, parts, final,
        load, sib_send, sib_recv, ring_send, ring_recv, one_send, one_recv, kv_send, kv_recv,
        dx_send, dx_recv, gn_send, gn_recv,
    ) = rest
    p = place()
    t = lax.axis_index("tensor")
    dp = lax.axis_index("dp")
    y, core = p["y"], p["c"]
    sibling = moved(p, "c", 1)
    every = slice(None)
    loads = []
    for lane, (at, rows, _) in enumerate(LANES):
        src = g_ref.at[:, core, :, :, :, pl.ds(at, rows), :]
        loads.append(pltpu.make_async_copy(src, acc.at[:, :, :, :, pl.ds(at, rows), :], load.at[lane]))
        loads[-1].start()
    gn_now[0] = gn_ref[...]
    greet(p)

    pending = []
    first = []
    for lane, (at, rows, _) in enumerate(LANES):
        src = g_ref.at[:, sibling["c"], :, :, :, pl.ds(at, rows), :]
        dst = other.at[:, :, :, :, pl.ds(at, rows), :]
        first.append(send(src, dst, sib_send.at[lane], sib_recv.at[lane], sibling))

    def dx_copy(k):
        return pltpu.make_async_remote_copy(
            src_ref=dx_ref.at[2 - k],
            dst_ref=dx_got.at[k - 1],
            send_sem=dx_send.at[k - 1],
            recv_sem=dx_recv.at[k - 1],
            device_id={"dp": dp, "tensor": jnp.maximum(t - k, 0)},
            device_id_type=MESH,
        )

    for k in (1, 2):
        @pl.when(t - k >= 0)
        def _(k=k):
            dx_copy(k).start()

    def pair(i):
        if i == 6:
            return sibling
        axis = "xyz"[i // 2]
        m = p[axis]
        q = dict(p)
        q[axis] = (m // 2) * 2 + (1 - m % 2) if i % 2 == 0 else 3 - m
        return q

    gn_copies = []

    def gn_start(i):
        gn_copies.append(send(gn_now.at[i], gn_got.at[i], gn_send.at[i], gn_recv.at[i], pair(i)))

    def gn_add(i):
        gn_copies[i].wait_recv()
        gn_now[i + 1] = gn_now[i] + gn_got[i]

    gn_start(0)
    for phase in (2, 1, 0):
        stage = 2 - phase
        step_one = []
        for lane, (at, rows, order) in enumerate(LANES):
            axis, gathered = order[phase], order[:phase]
            up, down = moved(p, axis, 1), moved(p, axis, 3)
            far = (p[axis] + 2) % 4
            b = bufs[lane * 9 + stage * 3 : lane * 9 + stage * 3 + 3]
            low, high = halves(at, rows)
            if stage == 0:
                loads[lane].wait()
                first[lane].wait_recv()
                for value in range(4):
                    add_blocks(
                        acc, p, axis, value, gathered, at, rows,
                        [slab(other, p, axis, value, gathered, at, rows)],
                    )
            sems = ring_send.at[lane, stage], ring_recv.at[lane, stage]
            low_buf = b[0].at[(slice(None),) * (len(b[0].shape) - 2) + (pl.ds(0, low[1]),)]
            high_buf = b[0].at[(slice(None),) * (len(b[0].shape) - 2) + (pl.ds(low[1], high[1]),)]
            one = send(slab(acc, p, axis, far, gathered, *low), low_buf, sems[0].at[0], sems[1].at[0], up)
            two = send(slab(acc, p, axis, far, gathered, *high), high_buf, sems[0].at[1], sems[1].at[1], down)
            step_one.append((one, two, low_buf, high_buf))
        gn_add(2 * stage)
        gn_start(2 * stage + 1)
        step_two = []
        for lane, (at, rows, order) in enumerate(LANES):
            axis, gathered = order[phase], order[:phase]
            up, down = moved(p, axis, 1), moved(p, axis, 3)
            b = bufs[lane * 9 + stage * 3 : lane * 9 + stage * 3 + 3]
            low, high = halves(at, rows)
            one, two, low_buf, high_buf = step_one[lane]
            sems = ring_send.at[lane, stage], ring_recv.at[lane, stage]
            one.wait_recv()
            add_blocks(acc, p, axis, up[axis], gathered, *low, [low_buf])
            three = send(slab(acc, p, axis, up[axis], gathered, at, rows), b[1], sems[0].at[2], sems[1].at[2], up)
            two.wait_recv()
            add_blocks(acc, p, axis, down[axis], gathered, *high, [high_buf])
            four = send(slab(acc, p, axis, down[axis], gathered, at, rows), b[2], sems[0].at[3], sems[1].at[3], down)
            step_two.append((three, four))
            pending += [one, two, three, four]
        gn_add(2 * stage + 1)
        gn_start(2 * stage + 2)
        for lane, (at, rows, order) in enumerate(LANES):
            axis, gathered = order[phase], order[:phase]
            b = bufs[lane * 9 + stage * 3 : lane * 9 + stage * 3 + 3]
            three, four = step_two[lane]
            three.wait_recv()
            four.wait_recv()
            add_blocks(acc, p, axis, p[axis], gathered, at, rows, [b[1], b[2]])

    mine = acc[p["x"] % 2, y, p["x"] // 2, p["z"]].astype(f32)
    for i, at in enumerate((0, G0, U0, D0)):
        for j in range(4):
            parts[j, 0:20, 128 * i : 128 * i + 128] = mine[at + 20 * j : at + 20 * j + 20]
    for j in range(4):
        parts[j, :, 512:640] = mine[KV0 : KV0 + 24]
    last = []
    for k in (1, 3, 2):
        q = moved(p, "y", k)
        last.append(send(parts.at[q["y"]], final.at[y], one_send.at[k - 1], one_recv.at[k - 1], q))
    final[pl.ds(y, 1)] = parts[pl.ds(y, 1)]
    gn_add(6)
    gn_out[...] = gn_now[7]
    for copy in last:
        copy.wait_recv()
    shard_ref[...] = final[:, :, :512]

    def kv_copy(k):
        return pltpu.make_async_remote_copy(
            src_ref=final.at[:, :, pl.ds(512, 128)],
            dst_ref=kv_ref,
            send_sem=kv_send.at[k - 1],
            recv_sem=kv_recv,
            device_id={"dp": dp, "tensor": (t + k) % 4},
            device_id_type=MESH,
        )

    @pl.when(t == y)
    def _():
        for k in (1, 2, 3):
            kv_copy(k).start()
        kv_ref[...] = final[:, :, 512:640]

    total = gx_ref[...]
    gx_out[...] = total
    for k in (1, 2):
        @pl.when(t + k <= 3)
        def _(k=k):
            dx_copy(k).wait_recv()
            gx_out[...] += dx_got[k - 1].astype(f32)

        @pl.when(t - k >= 0)
        def _(k=k):
            dx_copy(k).wait_send()

    for copy in first + pending + gn_copies + last:
        copy.wait_send()

    @pl.when(t == y)
    def _():
        for k in (1, 2, 3):
            kv_copy(k).wait_send()

    @pl.when(t != y)
    def _():
        kv_copy(1).wait_recv()


def reduce(grads, dx, gx, gn):
    dma = pltpu.SemaphoreType.DMA
    vmem = pl.BlockSpec(memory_space=pltpu.VMEM)
    hbm = pl.BlockSpec(memory_space=pl.ANY)
    bufs = []
    for _, rows, order in LANES:
        for phase in (2, 1, 0):
            shape = slab_shape(order[:phase], rows)
            bufs += [pltpu.VMEM(shape, bf16)] * 3
    return pl.pallas_call(
        reduce_kernel,
        out_shape=(
            jax.ShapeDtypeStruct((4, 24, 512), f32),
            jax.ShapeDtypeStruct((4, 24, 128), f32),
            jax.ShapeDtypeStruct((PART, D), f32),
            jax.ShapeDtypeStruct((8, D), f32),
        ),
        in_specs=[hbm, hbm, vmem, vmem],
        out_specs=(vmem,) * 4,
        scratch_shapes=[
            pltpu.VMEM((2, 4, 2, 4, BLOCK, 128), bf16),
            pltpu.VMEM((2, 4, 2, 4, BLOCK, 128), bf16),
            *bufs,
            pltpu.VMEM((2, PART, D), bf16),
            pltpu.VMEM((8, 8, D), f32),
            pltpu.VMEM((7, 8, D), f32),
            pltpu.VMEM((4, 24, D), f32),
            pltpu.VMEM((4, 24, D), f32),
            dma((3,)), dma((3,)), dma((3,)), dma((3, 3, 4)), dma((3, 3, 4)), dma((3,)), dma((3,)), dma((3,)), dma,
            dma((2,)), dma((2,)), dma((7,)), dma((7,)),
        ],
        compiler_params=pltpu.CompilerParams(
            collective_id=1, has_side_effects=True, vmem_limit_bytes=48 << 20
        ),
        name="reduce_gradients",
    )(grads, dx, gx, gn)


def window_rows(seg_ids, t):
    index = jnp.arange(seg_ids.shape[0], dtype=jnp.int32)
    n0 = jnp.sum((seg_ids == 0).astype(jnp.int32))
    n1 = jnp.sum((seg_ids <= 1).astype(jnp.int32))
    start = jnp.where(seg_ids == 0, 0, jnp.where(seg_ids == 1, n0, n1))
    positions = jnp.pad(index - start, (2 * PART, 0))
    positions = lax.dynamic_slice_in_dim(positions, t * PART, KEYS)
    low = jnp.maximum(index - (WINDOW - 1), start)
    low = lax.dynamic_slice_in_dim(low, t * PART, PART) - (t - 2) * PART
    return positions, low[:, None]


def shard_blocks(w_query, w_keyval, w_out, w_gate, w_up, w_down):
    out_t = w_out.T
    first = jnp.concatenate([w_query, out_t], axis=1)
    parts = [first, w_gate, w_up, w_down.T, w_keyval]
    rows = jnp.stack([item.reshape(20, 4, 128) for item in parts], axis=2)
    rows = jnp.moveaxis(rows.reshape(20, 4, 640), 1, 0)
    return jnp.pad(rows, ((0, 0), (0, 12), (0, 0)))


def per_device(
    tokens, segments, cotangent, w_query, w_keyval, w_out, w_gate, w_up, w_down,
    gain_in, gain_post_attn, gain_pre_ff, gain_post_ff, gain_query, gain_key,
):
    t = lax.axis_index("tensor")
    weights, x_parts = gather(shard_blocks(w_query, w_keyval, w_out, w_gate, w_up, w_down), tokens)
    positions, low = window_rows(segments[0], t)
    inv_freq = rope_base ** (-jnp.arange(0, HD, 2).astype(f32) / HD)
    angles = positions.astype(f32)[:, None] * inv_freq[None, :]
    gains = jnp.stack([gain_in, gain_post_attn, gain_pre_ff, gain_post_ff])
    head_gains = jnp.stack([gain_query, gain_key])
    output, gx, dx, grads, gn = layer(
        t.reshape(1), x_parts, cotangent, low, jnp.cos(angles), jnp.sin(angles), gains, head_gains,
        weights.reshape(CB, GROUPS, BLOCK, 128),
    )
    shard, kv, grad_x, gn = reduce(grads.reshape(2, 2, 4, 2, 4, BLOCK, 128), dx, gx, gn)
    rows = shard[:, :20].reshape(4, 20, 4, 128)
    first, gate, up, down = (jnp.moveaxis(rows[:, :, i], 0, 1).reshape(20, 512) for i in range(4))
    grad_kv = jnp.moveaxis(kv[:, :20], 0, 1).reshape(20, 512)
    return (
        output, grad_x, first[:, :256], grad_kv, first[:, 256:].T, gate, up, down.T,
        gn[0], gn[1], gn[2], gn[3], gn[4, :HD], gn[5, :HD],
    )


def solution(mesh):
    tok = P(("dp", "tensor"), None)
    weights = (
        P("dp", "tensor"), P("dp", None), P("tensor", "dp"), P("dp", "tensor"), P("dp", "tensor"), P("tensor", "dp"),
    )
    return jax.shard_map(
        per_device,
        mesh=mesh,
        in_specs=(tok, P("dp", None), tok) + weights + (P(),) * 6,
        out_specs=(tok, tok) + weights + (P(),) * 6,
        check_vma=False,
    )
```

time: 1230 us -> 184 us (0.15); the launches traced: 1210 us -> 183 us
  blocking collectives: 668 us -> 0 us
  waiting for transfers between devices: 296 us -> 0 us
  Pallas kernels: 0 us -> 152 us
  starting transfers between devices: 81.9 us -> 0 us
  matrix products: 65.9 us -> 0 us
  other arithmetic: 48.6 us -> 8.64 us
  between operations: 16.8 us -> 0.81 us
    all_gather x6 -> x0, blocking collectives: 484 us -> none  [the longest x1 87 us: per_device(): lax.all_gather(w_keyval, 'dp', axis=0, tiled=True)]
    reduce_scatter x4 -> x0, waiting for transfers between devices: 169 us -> none  [the longest x1 68.5 us: per_device(): lax.psum_scatter(jnp.dot(rows_here, out_full, preferred_element_type=jnp....]
    pallas_call x0 -> x3, Pallas kernels: none -> 152 us  [the longest x1 59.6 us: reduce(): pl.pallas_call(reduce_kernel, out_shape=(jax.ShapeDtypeStruct((4, 24, 512...]
    unnamed x1 -> x0, blocking collectives: 103 us -> none
    psum x1 -> x0, blocking collectives: 81.1 us -> none  [per_device(): lax.psum((keyval_part, gain_in_part, grad_gain_post_attn, grad_gain_pre_f...]
    unnamed x30 -> x0, starting transfers between devices: 81 us -> none
    psum x1 -> x0, waiting for transfers between devices: 79 us -> none  [per_device(): lax.psum((keyval_part, gain_in_part, grad_gain_post_attn, grad_gain_pre_f...]
    dot_general x32 -> x0, matrix products: 65.9 us -> none  [the longest x6 14.9 us: project_back(): lax.dot_general(grad_rows, weight_rows, (((1,), (1,)), ((), ())), preferr...]
  transfers between devices with their start and end apart: 39 -> 0, of which waited for: 6 -> 0; matrix products, arithmetic and copies ran while one was open for 10% -> 0% of each run, Pallas kernels for 0% -> 0%
where the time goes in v1:
time: 184 us; the launch traced here: 183 us
  Pallas kernels  152 us (83%)
  local copies, waits for them, and re-layouts  21.8 us (12%)
  other arithmetic  8.64 us (5%)
    pallas_call x1, Pallas kernels, reduce(): pl.pallas_call(reduce_kernel, out_shape=(jax.ShapeDtypeStruct((4, 24, 512...  59.6 us
    pallas_call x1, Pallas kernels, gather(): pl.pallas_call(gather_kernel, out_shape=(jax.ShapeDtypeStruct((2, 2, 4, 2...  53.1 us
    pallas_call x1, Pallas kernels, layer(): pl.pallas_call(layer_kernel, out_shape=(jax.ShapeDtypeStruct((PART, D), b...  39 us
    unnamed x27, local copies, waits for them, and re-layouts  12.7 us

profile of v1, /device:TPU:3, one launch (start us, length us, event | category | flops | bytes accessed | tf_op | source)
XLA Modules:
  0.0 183.0 jit_solution(665422039178251820)
XLA Ops:
  0.7 1.3 fusion.1
  2.0 1.3 pad_maximum_fusion.2.head_gains_ref
  3.3 0.7 stack.28
  4.0 0.7 stack.29
  4.7 0.7 stack.30
  5.3 0.7 stack.31
  6.0 0.6 pad_maximum_fusion.1.gains_ref
  6.7 2.0 %compare_select_fusion.1 = s32[1,1024]{1,0:T(1,128)S(1)} fusion(s32[1,1024]{1,0:T(1,128)} %param.16, s32[]{:T(128)} %get-tuple-element.41, s32[]{:T(128)} %get-tuple-element.40), kind=kLoop, calls=%fused_computation.9 | loop fusion | flops 4096 | bytes 8200 | tf_op jit(solution)/shard_map/jit(_where)/select_n | solution.py:750
  8.6 0.1 fusion
  8.7 0.1 dynamic-slice_subtract_fusion
  8.8 0.7 pad_maximum_fusion
  9.6 0.8 stack_reshape.24
  10.3 0.8 stack_reshape.21
  11.1 0.8 stack_reshape.22
  11.8 0.8 stack_reshape.23
  12.6 0.4 stack.27
  13.0 0.1 reshape.81
  13.1 0.8 copy.44.low_ref
  13.9 2.5 %multiply_sine_fusion = (f32[768,128]{1,0:T(8,128)}, f32[768,128]{1,0:T(8,128)}) fusion(f32[128]{0:T(128)S(1)} %multiply_power_fusion, f32[768]{0:T(1024)S(1)} %fusion), kind=kLoop, calls=%fused_computation | loop fusion | flops 98304 | bytes 790016 | tf_op jit(solution)/shard_map/sin | solution.py:779
  16.4 0.0 copy-start.4
  16.4 1.0 copy-done.4
  17.4 53.1 %gather_weights.1 = (bf16[2,2,4,2,4,352,128]{6,5,4,3,2,1,0:T(8,128)(2,1)S(1)}, bf16[3,256,640]{2,1,0:T(8,128)(2,1)S(1)}) custom-call(bf16[4,32,640]{2,1,0:T(8,128)(2,1)S(1)} %pad.8.s_ref, bf16[256,640]{1,0:T(8,128)(2,1)S(1)} %copy-done.4), custom_call_target="tpu_custom_call" | custom-call | tf_op jit(solution)/shard_map/gather_weights/pallas_call | solution.py:221
  70.5 0.0 copy-start
  70.5 4.3 %copy-done = bf16[2,2,4,2,4,352,128]{6,5,4,3,2,1,0:T(8,128)(2,1)} copy-done((bf16[2,2,4,2,4,352,128]{6,5,4,3,2,1,0:T(8,128)(2,1)}, bf16[2,2,4,2,4,352,128]{6,5,4,3,2,1,0:T(8,128)(2,1)S(1)}, u32[]{:S(2)}) %copy-start) | copy-done | bytes 11534360
  74.9 0.0 copy-start.1
  74.9 1.0 copy-done.1
  75.8 39.0 %layer.1 = (bf16[256,640]{1,0:T(8,128)(2,1)}, f32[256,640]{1,0:T(8,128)}, bf16[2,256,640]{2,1,0:T(8,128)(2,1)}, bf16[16,8,352,128]{3,2,1,0:T(8,128)(2,1)}, f32[8,640]{1,0:T(8,128)}) custom-call(s32[1]{0:T(128)} %bitcast.t_ref, bf16[3,256,640]{2,1,0:T(8,128)(2,1)} %copy-done.1, bf16[256,640]{1,0:T(8,128)(2,1)} %cot_ref.1, s32[256,1]{1,0:T(8,128)} %copy.44.low_ref, ...), custom_call_target="tpu_custom_call" | custom-call | tf_op jit(solution)/shard_map/layer/pallas_call | solution.py:454
  114.8 0.0 copy-start.2
  114.8 1.1 copy-done.2
  115.9 0.0 copy-start.3
  115.9 1.1 copy-done.3
  117.0 0.0 copy-start.5
  117.0 0.7 copy-done.5
  117.7 59.6 %reduce_gradients.1 = (f32[4,24,512]{2,1,0:T(8,128)S(1)}, f32[4,24,128]{2,1,0:T(8,128)S(1)}, f32[256,640]{1,0:T(8,128)S(1)}, f32[8,640]{1,0:T(8,128)S(1)}) custom-call(bf16[2,2,4,2,4,352,128]{6,5,4,3,2,1,0:T(8,128)(2,1)} %bitcast.50, bf16[2,256,640]{2,1,0:T(8,128)(2,1)S(1)} %copy-done.3, f32[256,640]{1,0:T(8,128)S(1)} %copy-done.2, f32[8,640]{1,0:T(8,128)S(1)} %copy-done.5), custom_call_target="tpu_custom_call" | custom-call | tf_op jit(solution)/shard_map/reduce_gradients/pallas_call | solution.py:717
  177.4 0.1 reshape.90
  177.5 0.1 fusion.3
  177.6 0.6 fusion.4
  178.2 0.6 slice_reduce_fusion
  178.8 0.6 copy.56
  179.5 0.6 copy.55
  180.2 0.6 copy.54
  180.9 0.6 slice_bitcast_fusion.1
  181.5 0.6 copy.53
  182.2 0.8 copy.60
  (17 shorter events, 0.3 us)
Async XLA Ops:
  16.4 1.0 copy-start.4
  70.5 4.4 %copy-start = (bf16[2,2,4,2,4,352,128]{6,5,4,3,2,1,0:T(8,128)(2,1)}, bf16[2,2,4,2,4,352,128]{6,5,4,3,2,1,0:T(8,128)(2,1)S(1)}, u32[]{:S(2)}) copy-start(bf16[2,2,4,2,4,352,128]{6,5,4,3,2,1,0:T(8,128)(2,1)S(1)} %get-tuple-element.26) | copy-start | bytes 34603012
  74.9 1.0 copy-start.1
  114.8 1.1 copy-start.2
  115.9 1.1 copy-start.3
  117.0 0.7 copy-start.5

commit v2 on v1

v2 whole, which is shorter than its diff:
```python
import jax
import jax.numpy as jnp
import numpy as np
from jax import lax
from jax.experimental import pallas as pl
from jax.experimental.pallas import tpu as pltpu
from jax.sharding import PartitionSpec as P

HD = 256
WINDOW = 512
D = 640
PART = 256
KEYS = 768
BLOCK = 352
CB = 16
GROUPS = 8
KV0, G0, U0, D0 = 80, 112, 192, 272
ATTN = ((0, 0, 48, "xyz"), (1, 48, 32, "yzx"), (2, 80, 32, "zxy"))
FEED = ((3, 112, 80, "xyz"), (4, 192, 80, "yzx"), (5, 272, 80, "zxy"))
LANES = ATTN + FEED
norm_eps = 1e-06
rope_base = 10000.0
MESH = pl.DeviceIdType.MESH
f32 = jnp.float32
bf16 = jnp.bfloat16


def place():
    dp = lax.axis_index("dp")
    t = lax.axis_index("tensor")
    return {
        "x": (dp // 16) * 2 + t // 2,
        "y": dp % 4,
        "z": (dp // 4) % 4,
        "c": t % 2,
    }


def device_of(p):
    return {
        "dp": (p["x"] // 2) * 16 + p["z"] * 4 + p["y"],
        "tensor": (p["x"] % 2) * 2 + p["c"],
    }


def moved(p, axis, by):
    size = 2 if axis == "c" else 4
    q = dict(p)
    q[axis] = (p[axis] + by) % size
    return q


def diagonal(p):
    q = moved(p, "c", 1)
    q["x"] = (p["x"] // 2) * 2 + (1 - p["x"] % 2)
    return q


def peers_of(p):
    found = [
        moved(p, axis, by)
        for axis, by in (("x", 1), ("x", 3), ("y", 1), ("y", 2), ("y", 3), ("z", 1), ("z", 3), ("c", 1))
    ]
    return found + [diagonal(p)]


def greet(p):
    barrier = pltpu.get_barrier_semaphore()
    peers = peers_of(p)
    for q in peers:
        pl.semaphore_signal(barrier, inc=1, device_id=device_of(q), device_id_type=MESH)
    pl.semaphore_wait(barrier, len(peers))


def send(src, dst, send_sem, recv_sem, q):
    copy = pltpu.make_async_remote_copy(
        src_ref=src,
        dst_ref=dst,
        send_sem=send_sem,
        recv_sem=recv_sem,
        device_id=device_of(q),
        device_id_type=MESH,
    )
    copy.start()
    return copy


def slab(ref, p, axis, value, gathered, first, rows, core=None):
    at = {a: (value if a == axis else p[a]) for a in "xyz"}
    every = slice(None)
    x_lo = every if "x" in gathered else at["x"] % 2
    x_hi = every if "x" in gathered else at["x"] // 2
    y = every if "y" in gathered else at["y"]
    z = every if "z" in gathered else at["z"]
    where = (x_lo,) + (() if core is None else (core,)) + (y, x_hi, z, pl.ds(first, rows), every)
    return ref.at[where]


def halves(first, rows):
    top = rows // 32 * 16 + (16 if rows % 32 else 0)
    return ((first, top), (first + top, rows - top))


def gather_steps(lanes, w_ref, p, sems):
    ring_send, ring_recv, sib_send, sib_recv = sems
    core = p["c"]
    sibling = moved(p, "c", 1)
    pending, to_sibling, passed = [], [], []

    def share(part, lane, i):
        to_sibling.append(send(part, part, sib_send.at[lane, i], sib_recv.at[lane, i], sibling))

    def arrived(phase):
        for i, (lane, at, rows, order) in enumerate(lanes):
            axis, gathered = order[phase], order[:phase]
            for j in range(2):
                passed[2 * i + j].wait_recv()
                if phase == 2:
                    far = (p[axis] + 2) % 4
                    share(slab(w_ref, p, axis, far, gathered, *halves(at, rows)[j], core), lane, 3 + j)
        pending.extend(passed)
        passed.clear()

    for phase in range(3):
        if phase:
            arrived(phase - 1)
        started = []
        for lane, at, rows, order in lanes:
            axis, gathered = order[phase], order[:phase]
            mine = slab(w_ref, p, axis, p[axis], gathered, at, rows, core)
            up, down = moved(p, axis, 1), moved(p, axis, 3)
            ss, rs = ring_send.at[lane, phase], ring_recv.at[lane, phase]
            started.append((send(mine, mine, ss.at[0], rs.at[0], up), send(mine, mine, ss.at[1], rs.at[1], down)))
            if phase == 2:
                share(mine, lane, 0)
        yield
        for (lane, at, rows, order), (to_up, to_down) in zip(lanes, started):
            axis, gathered = order[phase], order[:phase]
            up, down = moved(p, axis, 1), moved(p, axis, 3)
            ss, rs = ring_send.at[lane, phase], ring_recv.at[lane, phase]
            low, high = halves(at, rows)
            to_up.wait_recv()
            part = slab(w_ref, p, axis, down[axis], gathered, *low, core)
            passed.append(send(part, part, ss.at[2], rs.at[2], up))
            to_down.wait_recv()
            part = slab(w_ref, p, axis, up[axis], gathered, *high, core)
            passed.append(send(part, part, ss.at[3], rs.at[3], down))
            if phase == 2:
                for i, q in ((1, down), (2, up)):
                    share(slab(w_ref, p, axis, q[axis], gathered, at, rows, core), lane, i)
            pending.extend([to_up, to_down])
        yield
    arrived(2)
    for copy in to_sibling:
        copy.wait_recv()
    for copy in pending + to_sibling:
        copy.wait_send()
    yield


def slab_shape(gathered, rows):
    x = (2,) if "x" in gathered else ()
    y = (4,) if "y" in gathered else ()
    z = (4,) if "z" in gathered else ()
    return x + y + x + z + (rows, 128)


def add_blocks(acc, p, axis, value, gathered, first, rows, terms):
    sizes = slab_shape(gathered, rows)[:-2]
    count = 1
    for n in sizes:
        count *= n

    def step(i, _):
        index = []
        rest = i
        for n in reversed(sizes):
            index.append(rest % n)
            rest = rest // n
        index = index[::-1]
        at = iter(index)
        x_lo = next(at) if "x" in gathered else (value if axis == "x" else p["x"]) % 2
        y = next(at) if "y" in gathered else (value if axis == "y" else p["y"])
        x_hi = next(at) if "x" in gathered else (value if axis == "x" else p["x"]) // 2
        z = next(at) if "z" in gathered else (value if axis == "z" else p["z"])
        target = (x_lo, p["c"], y, x_hi, z, pl.ds(first, rows), slice(None))
        total = acc[target].astype(f32)
        for term in terms:
            total = total + term[tuple(index)].astype(f32)
        acc[target] = total.astype(bf16)
        return 0

    if count == 1:
        step(0, 0)
    else:
        lax.fori_loop(0, count, step, 0)


def reduce_steps(lanes, g_ref, other, bufs, p, sems):
    ring_send, ring_recv, sib_send, sib_recv = sems
    core = p["c"]
    sibling = moved(p, "c", 1)
    pending, from_sibling = [], {}
    for by in (2, 1, 3, 0):
        for lane, at, rows, order in lanes:
            axis, gathered = order[2], order[:2]
            value = (p[axis] + by) % 4
            src = slab(g_ref, p, axis, value, gathered, at, rows, sibling["c"])
            dst = slab(other, p, axis, value, gathered, at, rows)
            from_sibling[lane, by] = send(src, dst, sib_send.at[lane, by], sib_recv.at[lane, by], sibling)
    yield

    def sibling_part(lane, by, axis, gathered, at, rows):
        from_sibling[lane, by].wait_recv()
        return slab(other, p, axis, (p[axis] + by) % 4, gathered, at, rows)

    for stage in range(3):
        phase = 2 - stage
        one_step = []
        for lane, at, rows, order in lanes:
            axis, gathered = order[phase], order[:phase]
            up, down = moved(p, axis, 1), moved(p, axis, 3)
            far = (p[axis] + 2) % 4
            b = bufs[lane * 9 + stage * 3]
            low, high = halves(at, rows)
            if stage == 0:
                term = sibling_part(lane, 2, axis, gathered, at, rows)
                add_blocks(g_ref, p, axis, far, gathered, at, rows, [term])
            ss, rs = ring_send.at[lane, stage], ring_recv.at[lane, stage]
            lead = (slice(None),) * (len(b.shape) - 2)
            low_buf = b.at[lead + (pl.ds(0, low[1]), slice(None))]
            high_buf = b.at[lead + (pl.ds(low[1], high[1]), slice(None))]
            one = send(slab(g_ref, p, axis, far, gathered, *low, core), low_buf, ss.at[0], rs.at[0], up)
            two = send(slab(g_ref, p, axis, far, gathered, *high, core), high_buf, ss.at[1], rs.at[1], down)
            one_step.append((one, two, low_buf, high_buf))
        yield
        two_step = []
        for (lane, at, rows, order), (one, two, low_buf, high_buf) in zip(lanes, one_step):
            axis, gathered = order[phase], order[:phase]
            up, down = moved(p, axis, 1), moved(p, axis, 3)
            b = bufs[lane * 9 + stage * 3 : lane * 9 + stage * 3 + 3]
            low, high = halves(at, rows)
            ss, rs = ring_send.at[lane, stage], ring_recv.at[lane, stage]
            if stage == 0:
                for by, q in ((1, up), (3, down)):
                    term = sibling_part(lane, by, axis, gathered, at, rows)
                    add_blocks(g_ref, p, axis, q[axis], gathered, at, rows, [term])
            one.wait_recv()
            add_blocks(g_ref, p, axis, up[axis], gathered, *low, [low_buf])
            three = send(slab(g_ref, p, axis, up[axis], gathered, at, rows, core), b[1], ss.at[2], rs.at[2], up)
            two.wait_recv()
            add_blocks(g_ref, p, axis, down[axis], gathered, *high, [high_buf])
            four = send(slab(g_ref, p, axis, down[axis], gathered, at, rows, core), b[2], ss.at[3], rs.at[3], down)
            two_step.append((three, four))
            pending.extend([one, two, three, four])
        yield
        for (lane, at, rows, order), (three, four) in zip(lanes, two_step):
            axis, gathered = order[phase], order[:phase]
            b = bufs[lane * 9 + stage * 3 : lane * 9 + stage * 3 + 3]
            terms = [b[1], b[2]]
            if stage == 0:
                terms.append(sibling_part(lane, 0, axis, gathered, at, rows))
            three.wait_recv()
            four.wait_recv()
            add_blocks(g_ref, p, axis, p[axis], gathered, at, rows, terms)
        if stage == 2:
            for copy in pending + list(from_sibling.values()):
                copy.wait_send()
        yield


def dot(a, b):
    return jnp.dot(a, b, preferred_element_type=f32)


def dot_nt(a, b):
    return lax.dot_general(a, b, (((1,), (1,)), ((), ())), preferred_element_type=f32)


def inv_rms(v):
    return lax.rsqrt(jnp.mean(v * v, axis=-1, keepdims=True) + norm_eps)


def norm_back(v, r, c, e):
    ec = e * c
    vr = v * r
    dv = r * (ec - vr * jnp.mean(vr * ec, axis=-1, keepdims=True))
    return dv, jnp.sum(e * vr, axis=0, keepdims=True)


def turn(u, cos, sin):
    a, b = u[:, :128], u[:, 128:]
    return jnp.concatenate([a * cos - b * sin, b * cos + a * sin], axis=1)


def turn_back(e, cos, sin):
    a, b = e[:, :128], e[:, 128:]
    return jnp.concatenate([a * cos + b * sin, b * cos - a * sin], axis=1)


def columns(w_ref, t, y, first):
    return jnp.concatenate(
        [w_ref[t // 2, t % 2, y + i, :, :, first : first + 80, :].reshape(D, 128) for i in range(2)], axis=1
    )


def put_columns(g_ref, t, y, first, value):
    value = value.astype(bf16)
    for i in range(2):
        g_ref[t // 2, t % 2, y + i, :, :, first : first + 80, :] = (
            value[:, 128 * i : 128 * i + 128].reshape(2, 4, 80, 128)
        )


NB = 9 * len(LANES)


def kernel(
    seg_ref, wq_ref, wkv_ref, wo_ref, wg_ref, wu_ref, wd_ref, x_ref, cot_ref,
    gin_ref, gpa_ref, gpf_ref, gpo_ref, gq_ref, gk_ref, cos_tab, sin_tab, freq_ref,
    out_ref, gx_ref, shard_ref, kv_ref, gn_out,
    *scratch,
):
    bufs, scratch = scratch[:NB], scratch[NB:]
    (
        w_ref, g_ref, other, xg, rows_s, s_ref, got, stage,
        cos_ref, sin_ref, wkv, attn_in, attn_in_t, kt, vt, kb, vb, qraw, qb, probs, ctx,
        mlp_in, mlp_in_t, d_b, d_t, act_s, dact_s, hid_s, acc, acc2, dkt, dvt, proj_s,
        dx_got, gn_now, gn_got, final,
        one_send, one_recv, ring_send, ring_recv, sib_send, sib_recv, x_send, x_recv,
        back_send, back_recv, bsib_send, bsib_recv, last_send, last_recv, kv_send, kv_recv,
        dx_send, dx_recv, gn_send, gn_recv,
    ) = scratch
    p = place()
    t = lax.axis_index("tensor")
    dp = lax.axis_index("dp")
    y = p["y"]
    core = p["c"]
    own = (p["x"] % 2, core, y, p["x"] // 2, p["z"])
    greet(p)

    rows_s[...] = jnp.zeros_like(rows_s)
    out_t = wo_ref[...].astype(f32).T
    down_t = wd_ref[...].astype(f32).T
    for j in range(4):
        if j < 2:
            rows_s[j, :20, :128] = wq_ref[:, 128 * j : 128 * j + 128].astype(f32)
        else:
            rows_s[j, :20, :128] = out_t[:, 128 * j - 256 : 128 * j - 128]
        rows_s[j, :20, 128:256] = wg_ref[:, 128 * j : 128 * j + 128].astype(f32)
        rows_s[j, :20, 256:384] = wu_ref[:, 128 * j : 128 * j + 128].astype(f32)
        rows_s[j, :20, 384:512] = down_t[:, 128 * j : 128 * j + 128]
        rows_s[j, :20, 512:] = wkv_ref[:, 128 * j : 128 * j + 128].astype(f32)
    s_ref[...] = rows_s[...].astype(bf16)
    first = []
    for k in (1, 3, 2):
        q = moved(p, "y", k)
        first.append(send(s_ref.at[q["y"]], got.at[y], one_send.at[k - 1], one_recv.at[k - 1], q))

    def token_copy(src, slot, to):
        return pltpu.make_async_remote_copy(
            src_ref=src, dst_ref=xg.at[slot], send_sem=x_send.at[1 - slot], recv_sem=x_recv.at[1 - slot],
            device_id={"dp": dp, "tensor": to}, device_id_type=MESH,
        )

    @pl.when(t < 3)
    def _():
        token_copy(x_ref, 1, jnp.minimum(t + 1, 3)).start()

    @pl.when(t == 0)
    def _():
        token_copy(x_ref, 0, t + 2).start()

    xg[2] = x_ref[...]
    got[pl.ds(y, 1)] = s_ref[pl.ds(y, 1)]
    for copy in first:
        copy.wait_recv()
    for j in range(4):
        stage[20 * j : 20 * j + 20, :] = got[j].astype(f32)[:20, :512]
    for i, at in enumerate((0, G0, U0, D0)):
        w_ref[own + (slice(at, at + 80),)] = stage[:80, 128 * i : 128 * i + 128].astype(bf16)
    w_ref[own + (slice(KV0, KV0 + 32),)] = got[pl.ds(t, 1)][0, :, 512:640]
    for copy in first:
        copy.wait_send()

    sems = (ring_send, ring_recv, sib_send, sib_recv)
    attn = gather_steps(ATTN, w_ref, p, sems)
    feed = gather_steps(FEED, w_ref, p, sems)
    for _ in range(2):
        next(attn), next(feed)
    for _ in range(2):
        next(attn), next(feed)
    next(attn)

    gin, gpa, gpf, gpo, gq, gk = (
        ref[...].reshape(1, ref.shape[0]) for ref in (gin_ref, gpa_ref, gpf_ref, gpo_ref, gq_ref, gk_ref)
    )
    scale = HD ** -0.5
    seg = seg_ref[...]
    n0 = jnp.sum(jnp.where(seg == 0, 1.0, 0.0), axis=1, keepdims=True)
    n1 = jnp.sum(jnp.where(seg <= 1, 1.0, 0.0), axis=1, keepdims=True)
    base = ((t - 2) * PART).astype(f32)
    which = lax.broadcasted_iota(jnp.int32, (8, 128), 0)
    turn_by = (jnp.where(which == 0, 0.0, jnp.where(which == 1, n0, n1)) - base) * freq_ref[...]
    cb, sb = jnp.cos(turn_by), jnp.sin(turn_by)
    token = lax.broadcasted_iota(jnp.int32, (KEYS, 1), 0).astype(f32) + base
    in0, in1 = token < n0, token < n1
    cd = jnp.where(in0, cb[0:1], jnp.where(in1, cb[1:2], cb[2:3]))
    sd = jnp.where(in0, sb[0:1], jnp.where(in1, sb[1:2], sb[2:3]))
    ca, sa = cos_tab[...], sin_tab[...]
    cos_ref[...] = ca * cd + sa * sd
    sin_ref[...] = sa * cd - ca * sd

    @pl.when(t > 0)
    def _():
        token_copy(x_ref, 1, jnp.minimum(t + 1, 3)).wait_recv()

    @pl.when(t == 2)
    def _():
        token_copy(xg.at[1], 0, jnp.minimum(t + 1, 3)).start()

    @pl.when(t >= 2)
    def _():
        token_copy(x_ref, 0, jnp.minimum(t + 1, 3)).wait_recv()

    @pl.when(t < 3)
    def _():
        token_copy(x_ref, 1, jnp.minimum(t + 1, 3)).wait_send()

    @pl.when(lax.rem(t, 2) == 0)
    def _():
        token_copy(x_ref, 0, jnp.minimum(t + 1, 3)).wait_send()

    def tokens(i):
        return jnp.where(i >= 2 - t, xg[i].astype(f32), 0.0)

    def input_norm(i, _):
        x = tokens(i)
        a = x * inv_rms(x) * gin
        attn_in[i] = a.astype(bf16)
        attn_in_t[i] = a.T.astype(bf16)
        return 0

    lax.fori_loop(0, 3, input_norm, 0)
    acc[...] = jnp.zeros_like(acc)
    next(attn)
    next(feed)
    next(attn)

    def keyval_in(g, _):
        for tt in range(4):
            for yy in range(4):
                stage[20 * tt : 20 * tt + 20, 128 * yy : 128 * yy + 128] = (
                    w_ref[tt // 2, tt % 2, yy, g // 4, g % 4, KV0 : KV0 + 32, :].astype(f32)[:20]
                )
        wkv[g] = stage[:80, :].astype(bf16)
        return 0

    lax.fori_loop(0, GROUPS, keyval_in, 0)

    def rows_of(i):
        return pl.ds(pl.multiple_of(i * PART, PART), PART)

    def keys_values(i, _):
        rows = rows_of(i)
        kv_raw = dot(attn_in[i], wkv[...].reshape(D, 512))
        kraw = kv_raw[:, :HD]
        k = turn(kraw * inv_rms(kraw) * gk, cos_ref[rows, :], sin_ref[rows, :])
        kb[rows, :] = k.astype(bf16)
        kt[:, rows] = k.T.astype(bf16)
        v = kv_raw[:, HD:]
        vb[rows, :] = v.astype(bf16)
        vt[:, rows] = v.T.astype(bf16)
        return 0

    lax.fori_loop(0, 3, keys_values, 0)

    def head(h, _):
        cos_q, sin_q = cos_ref[2 * PART :, :], sin_ref[2 * PART :, :]
        column = lax.broadcasted_iota(jnp.int32, (PART, KEYS), 1)
        last = lax.broadcasted_iota(jnp.int32, (PART, 1), 0) + 2 * PART
        own_token = last.astype(f32) + base
        start = jnp.where(own_token < n0, 0.0, jnp.where(own_token < n1, n0, n1))
        low = jnp.maximum(own_token - (WINDOW - 1), start) - base
        raw = dot(attn_in[2], columns(w_ref, h, 0, 0))
        qraw[h] = raw
        q = turn(raw * inv_rms(raw) * gq, cos_q, sin_q).astype(bf16)
        qb[h] = q
        s = dot(q, kt[...]) * scale
        s = jnp.where((column.astype(f32) >= low) & (column <= last), s, -1e30)
        e = jnp.exp(s - jnp.max(s, axis=-1, keepdims=True))
        pr = e / jnp.sum(e, axis=-1, keepdims=True)
        probs[h] = pr
        c = dot(pr.astype(bf16), vb[...]).astype(bf16)
        ctx[h] = c
        acc[...] += dot_nt(c, columns(w_ref, h, 2, 0))
        return 0

    lax.fori_loop(0, 3, head, 0)
    next(feed)
    lax.fori_loop(3, 4, head, 0)
    proj = acc[...]
    proj_s[...] = proj
    mid = x_ref[...].astype(f32) + proj * inv_rms(proj) * gpa
    gx_ref[...] = mid
    m = mid * inv_rms(mid) * gpf
    mlp_in[...] = m.astype(bf16)
    mlp_in_t[...] = m.T.astype(bf16)
    acc[...] = jnp.zeros_like(acc)
    next(feed)

    def feed_forward(c, _):
        tt, yy = c // 2, 2 * (c % 2)
        gate = dot(mlp_in[...], columns(w_ref, tt, yy, G0))
        up = dot(mlp_in[...], columns(w_ref, tt, yy, U0))
        k0, k1 = 0.7978845608028654, 0.044715
        sq = gate * gate
        th = jnp.tanh(k0 * (gate + k1 * gate * sq))
        half = 0.5 * (1.0 + th)
        act = gate * half
        hid = (act * up).astype(bf16)
        act_s[c] = act
        dact_s[c] = up * (half + 0.5 * gate * (1.0 - th * th) * (k0 + (3.0 * k0 * k1) * sq))
        hid_s[c] = hid
        acc[...] += dot_nt(hid, columns(w_ref, tt, yy, D0))
        return 0

    lax.fori_loop(0, 8, feed_forward, 0)
    mlp = acc[...]
    r = inv_rms(mlp)
    out_ref[...] = (gx_ref[...] + mlp * r * gpo).astype(bf16)
    d_mlp, g_po = norm_back(mlp, r, gpo, cot_ref[...].astype(f32))
    gn_now[0, 3:4, :] = g_po
    d_b[...] = d_mlp.astype(bf16)
    d_t[...] = d_mlp.T.astype(bf16)
    acc[...] = jnp.zeros_like(acc)

    def feed_back(c, _):
        tt, yy = c // 2, 2 * (c % 2)
        put_columns(g_ref, tt, yy, D0, dot(d_t[...], hid_s[c]))
        d_hid = dot(d_b[...], columns(w_ref, tt, yy, D0))
        d_gate = (d_hid * dact_s[c]).astype(bf16)
        d_up = (d_hid * act_s[c]).astype(bf16)
        put_columns(g_ref, tt, yy, G0, dot(mlp_in_t[...], d_gate))
        put_columns(g_ref, tt, yy, U0, dot(mlp_in_t[...], d_up))
        acc[...] += dot_nt(d_gate, columns(w_ref, tt, yy, G0)) + dot_nt(d_up, columns(w_ref, tt, yy, U0))
        return 0

    lax.fori_loop(0, 8, feed_back, 0)
    sems = (back_send, back_recv, bsib_send, bsib_recv)
    feed = reduce_steps(FEED, g_ref, other, bufs, p, sems)
    next(feed)

    mid = gx_ref[...]
    d_pre, g_pf = norm_back(mid, inv_rms(mid), gpf, acc[...])
    gn_now[0, 2:3, :] = g_pf
    d_mid = cot_ref[...].astype(f32) + d_pre
    proj = proj_s[...]
    d_proj, g_pa = norm_back(proj, inv_rms(proj), gpa, d_mid)
    gn_now[0, 1:2, :] = g_pa
    gx_ref[...] = d_mid
    d_b[...] = d_proj.astype(bf16)
    d_t[...] = d_proj.T.astype(bf16)
    dkt[...] = jnp.zeros_like(dkt)
    dvt[...] = jnp.zeros_like(dvt)
    acc[...] = jnp.zeros_like(acc)
    acc2[...] = jnp.zeros_like(acc2)
    next(feed)

    def head_back(h, _):
        cos_q, sin_q = cos_ref[2 * PART :, :], sin_ref[2 * PART :, :]
        put_columns(g_ref, h, 2, 0, dot(d_t[...], ctx[h]))
        d_ctx = dot(d_b[...], columns(w_ref, h, 2, 0))
        d_ctx_b = d_ctx.astype(bf16)
        pr = probs[h]
        d_pr = dot(d_ctx_b, vt[...])
        dvt[...] += dot(d_ctx.T.astype(bf16), pr.astype(bf16))
        inner = jnp.sum(pr * d_pr, axis=-1, keepdims=True)
        ds = (pr * (d_pr - inner)).astype(bf16)
        dq = dot(ds, kb[...]) * scale
        dkt[...] += dot(qb[h].astype(f32).T.astype(bf16), ds)
        raw = qraw[h]
        d_raw, g_q = norm_back(raw, inv_rms(raw), gq, turn_back(dq, cos_q, sin_q))
        acc2[...] += g_q
        d_raw = d_raw.astype(bf16)
        put_columns(g_ref, h, 0, 0, dot(attn_in_t[2], d_raw))
        acc[...] += dot_nt(d_raw, columns(w_ref, h, 0, 0))
        return 0

    lax.fori_loop(0, 2, head_back, 0)
    next(feed)
    lax.fori_loop(2, 4, head_back, 0)
    gn_now[0, 4:8, :] = jnp.zeros((4, D), f32)
    gn_now[0, 4:5, :HD] = acc2[...]
    acc2[...] = jnp.zeros_like(acc2)

    def keys_values_back(i, _):
        rows = rows_of(i)
        raw = dot(attn_in[i], wkv[:, :, :HD].reshape(D, HD))
        e = turn_back(dkt[:, rows].T * scale, cos_ref[rows, :], sin_ref[rows, :])
        dk, g_k = norm_back(raw, inv_rms(raw), gk, e)
        acc2[...] += g_k
        kb[rows, :] = dk.astype(bf16)
        vb[rows, :] = dvt[:, rows].T.astype(bf16)
        return 0

    lax.fori_loop(0, 3, keys_values_back, 0)
    gn_now[0, 5:6, :HD] = acc2[...]
    for half, src in enumerate((kb, vb)):
        grad = sum(dot(attn_in_t[i], src[PART * i : PART * i + PART, :]) for i in range(3))
        stage[80:, :] = jnp.zeros((16, 512), f32)
        for g in range(GROUPS):
            stage[:80, :HD] = grad[80 * g : 80 * g + 80]
            for tt in range(4):
                for yy in range(2):
                    g_ref[tt // 2, tt % 2, 2 * half + yy, g // 4, g % 4, KV0 : KV0 + 32, :] = (
                        stage[20 * tt : 20 * tt + 32, 128 * yy : 128 * yy + 128].astype(bf16)
                    )
    attn = reduce_steps(ATTN, g_ref, other, bufs, p, sems)
    next(attn)

    def input_back(i, extra):
        rows = rows_of(i)
        d_in = dot_nt(kb[rows, :], wkv[:, :, :HD].reshape(D, HD)) + dot_nt(vb[rows, :], wkv[:, :, HD:].reshape(D, HD))
        x = tokens(i)
        dx, g_in = norm_back(x, inv_rms(x), gin, d_in if extra is None else d_in + extra)
        gn_now[0, 0:1, :] += g_in
        return dx

    def input_back_before(i, _):
        attn_in[i] = input_back(i, None).astype(bf16)
        return 0

    gn_now[0, 0:1, :] = jnp.zeros((1, D), f32)
    lax.fori_loop(0, 2, input_back_before, 0)
    gx_ref[...] += input_back(2, acc[...])

    def dx_copy(k):
        return pltpu.make_async_remote_copy(
            src_ref=attn_in.at[2 - k], dst_ref=dx_got.at[k - 1], send_sem=dx_send.at[k - 1], recv_sem=dx_recv.at[k - 1],
            device_id={"dp": dp, "tensor": jnp.maximum(t - k, 0)}, device_id_type=MESH,
        )

    for k in (1, 2):
        @pl.when(t - k >= 0)
        def _(k=k):
            dx_copy(k).start()

    def pair(i):
        if i == 6:
            return moved(p, "c", 1)
        axis = "xyz"[i // 2]
        m = p[axis]
        q = dict(p)
        q[axis] = (m // 2) * 2 + (1 - m % 2) if i % 2 == 0 else 3 - m
        return q

    gn_copies = []

    def gn_start(i):
        gn_copies.append(send(gn_now.at[i], gn_got.at[i], gn_send.at[i], gn_recv.at[i], pair(i)))

    def gn_add(i):
        gn_copies[i].wait_recv()
        gn_now[i + 1] = gn_now[i] + gn_got[i]

    gn_start(0)
    next(attn)
    next(feed)
    next(feed)
    gn_add(0)
    gn_start(1)
    next(attn)
    next(feed)
    gn_add(1)
    gn_start(2)
    next(attn)
    next(attn)
    next(feed)
    next(feed)
    gn_add(2)
    gn_start(3)
    next(attn)
    next(feed)
    gn_add(3)
    gn_start(4)
    next(attn)
    next(attn)
    next(feed)
    gn_add(4)
    gn_start(5)
    next(attn)
    gn_add(5)
    gn_start(6)
    next(attn)

    mine = g_ref[own].astype(f32)
    for i, at in enumerate((0, G0, U0, D0)):
        for j in range(4):
            rows_s[j, 0:20, 128 * i : 128 * i + 128] = mine[at + 20 * j : at + 20 * j + 20]
    for j in range(4):
        rows_s[j, :24, 512:] = mine[KV0 : KV0 + 24]
    last = []
    for k in (1, 3, 2):
        q = moved(p, "y", k)
        last.append(send(rows_s.at[q["y"], pl.ds(0, 24), :], final.at[y], last_send.at[k - 1], last_recv.at[k - 1], q))
    final[pl.ds(y, 1)] = rows_s[pl.ds(y, 1), :24]
    gn_add(6)
    gn_out[...] = gn_now[7]
    for k in (1, 2):
        @pl.when(t + k <= 3)
        def _(k=k):
            dx_copy(k).wait_recv()
            gx_ref[...] += dx_got[k - 1].astype(f32)

        @pl.when(t - k >= 0)
        def _(k=k):
            dx_copy(k).wait_send()

    for copy in last:
        copy.wait_recv()

    def kv_copy(k):
        return pltpu.make_async_remote_copy(
            src_ref=final.at[:, :, pl.ds(512, 128)], dst_ref=kv_ref, send_sem=kv_send.at[k - 1], recv_sem=kv_recv,
            device_id={"dp": dp, "tensor": (t + k) % 4}, device_id_type=MESH,
        )

    @pl.when(t == y)
    def _():
        for k in (1, 2, 3):
            kv_copy(k).start()
        kv_ref[...] = final[:, :, 512:640]

    shard_ref[...] = final[:, :, :512]
    for copy in gn_copies + last:
        copy.wait_send()

    @pl.when(t == y)
    def _():
        for k in (1, 2, 3):
            kv_copy(k).wait_send()

    @pl.when(t != y)
    def _():
        kv_copy(1).wait_recv()


def layer(*args):
    dma = pltpu.SemaphoreType.DMA
    vmem = pl.BlockSpec(memory_space=pltpu.VMEM)
    bufs = []
    for _, _, rows, order in LANES:
        for phase in (2, 1, 0):
            bufs += [pltpu.VMEM(slab_shape(order[:phase], rows), bf16)] * 3
    n = len(LANES)
    return pl.pallas_call(
        kernel,
        out_shape=(
            jax.ShapeDtypeStruct((PART, D), bf16),
            jax.ShapeDtypeStruct((PART, D), f32),
            jax.ShapeDtypeStruct((4, 24, 512), f32),
            jax.ShapeDtypeStruct((4, 24, 128), f32),
            jax.ShapeDtypeStruct((8, D), f32),
        ),
        in_specs=[vmem] * len(args),
        out_specs=(vmem,) * 5,
        scratch_shapes=[
            *bufs,
            pltpu.VMEM((2, 2, 4, 2, 4, BLOCK, 128), bf16),
            pltpu.VMEM((2, 2, 4, 2, 4, BLOCK, 128), bf16),
            pltpu.VMEM((2, 4, 2, 4, BLOCK, 128), bf16),
            pltpu.VMEM((3, PART, D), bf16),
            pltpu.VMEM((4, 32, D), f32),
            pltpu.VMEM((4, 32, D), bf16),
            pltpu.VMEM((4, 32, D), bf16),
            pltpu.VMEM((96, 512), f32),
            pltpu.VMEM((KEYS, 128), f32),
            pltpu.VMEM((KEYS, 128), f32),
            pltpu.VMEM((GROUPS, 80, 512), bf16),
            pltpu.VMEM((3, PART, D), bf16),
            pltpu.VMEM((3, D, PART), bf16),
            pltpu.VMEM((HD, KEYS), bf16),
            pltpu.VMEM((HD, KEYS), bf16),
            pltpu.VMEM((KEYS, HD), bf16),
            pltpu.VMEM((KEYS, HD), bf16),
            pltpu.VMEM((4, PART, HD), f32),
            pltpu.VMEM((4, PART, HD), bf16),
            pltpu.VMEM((4, PART, KEYS), f32),
            pltpu.VMEM((4, PART, HD), bf16),
            pltpu.VMEM((PART, D), bf16),
            pltpu.VMEM((D, PART), bf16),
            pltpu.VMEM((PART, D), bf16),
            pltpu.VMEM((D, PART), bf16),
            pltpu.VMEM((8, PART, 256), f32),
            pltpu.VMEM((8, PART, 256), f32),
            pltpu.VMEM((8, PART, 256), bf16),
            pltpu.VMEM((PART, D), f32),
            pltpu.VMEM((1, HD), f32),
            pltpu.VMEM((HD, KEYS), f32),
            pltpu.VMEM((HD, KEYS), f32),
            pltpu.VMEM((PART, D), f32),
            pltpu.VMEM((2, PART, D), bf16),
            pltpu.VMEM((8, 8, D), f32),
            pltpu.VMEM((7, 8, D), f32),
            pltpu.VMEM((4, 24, D), f32),
            dma((3,)), dma((3,)), dma((n, 3, 4)), dma((n, 3, 4)), dma((n, 5)), dma((n, 5)), dma((2,)), dma((2,)),
            dma((n, 3, 4)), dma((n, 3, 4)), dma((n, 4)), dma((n, 4)), dma((3,)), dma((3,)), dma((3,)), dma,
            dma((2,)), dma((2,)), dma((7,)), dma((7,)),
        ],
        compiler_params=pltpu.CompilerParams(
            collective_id=0, has_side_effects=True, vmem_limit_bytes=62 << 20
        ),
        name="layer",
    )(*args)


def rope_parts():
    freq = (rope_base ** (-np.arange(0, HD, 2, dtype=np.float64) / HD))[None, :]
    angles = np.arange(KEYS, dtype=np.float64)[:, None] * freq
    return tuple(jnp.asarray(item.astype(np.float32)) for item in (np.cos(angles), np.sin(angles), freq))


def per_device(
    tokens, segments, cotangent, w_query, w_keyval, w_out, w_gate, w_up, w_down,
    gain_in, gain_post_attn, gain_pre_ff, gain_post_ff, gain_query, gain_key,
):
    output, grad_x, shard, kv, gn = layer(
        segments, w_query, w_keyval, w_out, w_gate, w_up, w_down, tokens, cotangent,
        gain_in, gain_post_attn, gain_pre_ff, gain_post_ff, gain_query, gain_key, *rope_parts(),
    )
    rows = shard[:, :20].reshape(4, 20, 4, 128)
    first, gate, up, down = (jnp.moveaxis(rows[:, :, i], 0, 1).reshape(20, 512) for i in range(4))
    grad_kv = jnp.moveaxis(kv[:, :20], 0, 1).reshape(20, 512)
    return (
        output, grad_x, first[:, :256], grad_kv, first[:, 256:].T, gate, up, down.T,
        gn[0], gn[1], gn[2], gn[3], gn[4, :HD], gn[5, :HD],
    )


def solution(mesh):
    tok = P(("dp", "tensor"), None)
    weights = (
        P("dp", "tensor"), P("dp", None), P("tensor", "dp"), P("dp", "tensor"), P("dp", "tensor"), P("tensor", "dp"),
    )
    return jax.shard_map(
        per_device,
        mesh=mesh,
        in_specs=(tok, P("dp", None), tok) + weights + (P(),) * 6,
        out_specs=(tok, tok) + weights + (P(),) * 6,
        check_vma=False,
    )
```

time: 184 us -> 151 us (0.82)
  Pallas kernels: 152 us -> 139 us
  local copies, waits for them, and re-layouts: 21.8 us -> 10.5 us
  other arithmetic: 8.64 us -> 0 us
    pallas_call x3 -> x1, Pallas kernels: 152 us -> 139 us  [layer(): pl.pallas_call(kernel, out_shape=(jax.ShapeDtypeStruct((PART, D), bf16),...]
    another operation x10 -> x0, local copies, waits for them, and re-layouts: 6.18 us -> none  [the longest x6 3.43 us: shard_blocks(): rows = jnp.stack([item.reshape(20, 4, 128) for item in parts], axis=2)]
    unnamed x27 -> x28, local copies, waits for them, and re-layouts: 12.7 us -> 6.76 us
    sin x1 -> x0, other arithmetic: 2.52 us -> none  [per_device(): jnp.sin(angles)]
    select_n x1 -> x0, other arithmetic: 1.99 us -> none  [window_rows(): start = jnp.where(seg_ids == 0, 0, jnp.where(seg_ids == 1, n0, n1))]
    another operation x2 -> x0, other arithmetic: 1.89 us -> none  [the longest x1 1.28 us: per_device(): head_gains = jnp.stack([gain_query, gain_key])]
where the time goes in v2:
time: 151 us; the launch traced here: 150 us
  Pallas kernels  139 us (92%)
  local copies, waits for them, and re-layouts  10.5 us (7%)
    pallas_call x1, Pallas kernels, layer(): pl.pallas_call(kernel, out_shape=(jax.ShapeDtypeStruct((PART, D), bf16),...  139 us
    unnamed x28, local copies, waits for them, and re-layouts  6.76 us

profile of v2, /device:TPU:3, one launch (start us, length us, event | category | flops | bytes accessed | tf_op | source)
XLA Modules:
  0.0 150.2 jit_solution(15559490494936028884)
XLA Ops:
  0.6 0.0 copy-start.4
  0.7 1.5 copy.38.wo_ref
  2.1 0.0 copy-done.4
  2.1 0.8 copy.39.wd_ref
  2.9 138.9 %layer.1 = (bf16[256,640]{1,0:T(8,128)(2,1)}, f32[256,640]{1,0:T(8,128)}, f32[4,24,512]{2,1,0:T(8,128)}, f32[4,24,128]{2,1,0:T(8,128)}, f32[8,640]{1,0:T(8,128)}) custom-call(s32[1,1024]{1,0:T(1,128)} %seg_ref.1, bf16[20,256]{1,0:T(8,128)(2,1)} %wq_ref.1, bf16[20,512]{1,0:T(8,128)(2,1)} %wkv_ref.1, bf16[256,20]{1,0:T(8,128)(2,1)} %copy.38.wo_ref, ...), custom_call_target="tpu_custom_call" | custom-call | tf_op jit(solution)/shard_map/layer/pallas_call | solution.py:757
  141.8 0.0 copy-start.3
  141.8 1.3 fusion.1
  143.2 1.6 %slice_reduce_fusion = (f32[640]{0:T(1024)}, f32[640]{0:T(1024)}, f32[640]{0:T(1024)}, f32[640]{0:T(1024)}) fusion(f32[8,640]{1,0:T(8,128)} %get-tuple-element.23), kind=kLoop, calls=%fused_computation.2 | loop fusion | bytes 20480 | tf_op jit(solution)/shard_map/slice | solution.py:837
  144.8 0.0 copy-start.2
  144.8 0.0 copy-done.3
  144.8 0.6 copy.48
  145.4 0.3 copy-done.2
  145.7 0.1 reshape.52
  145.8 0.1 fusion
  145.9 0.6 copy.51
  146.6 0.6 copy.50
  147.2 0.0 copy-start.1
  147.2 0.0 copy-start
  147.3 0.6 copy.49
  148.0 0.6 slice_bitcast_fusion.1
  148.6 0.0 copy-done.1
  148.6 0.7 copy.54
  149.3 0.0 copy-done
  149.3 0.8 copy.55
  (12 shorter events, 0.2 us)
Async XLA Ops:
  0.6 1.5 copy-start.4
  141.8 2.9 %copy-start.3 = (f32[4,24,128]{2,1,0:T(8,128)S(1)}, f32[4,24,128]{2,1,0:T(8,128)}, u32[]{:S(2)}) copy-start(f32[4,24,128]{2,1,0:T(8,128)} %get-tuple-element.22) | copy-start | bytes 147460
  144.8 0.9 copy-start.2
  147.2 1.4 copy-start.1
  147.2 2.1 %copy-start = (f32[256,640]{1,0:T(8,128)S(1)}, f32[256,640]{1,0:T(8,128)}, u32[]{:S(2)}) copy-start(f32[256,640]{1,0:T(8,128)} %get-tuple-element.51) | copy-start | bytes 1966084

commit v3 on v2

--- a/solution.py
+++ b/solution.py
@@ -59,7 +59,9 @@
 def peers_of(p):
     found = [
         moved(p, axis, by)
-        for axis, by in (("x", 1), ("x", 3), ("y", 1), ("y", 2), ("y", 3), ("z", 1), ("z", 3), ("c", 1))
+        for axis, by in (
+            ("x", 1), ("x", 2), ("x", 3), ("y", 1), ("y", 2), ("y", 3), ("z", 1), ("z", 2), ("z", 3), ("c", 1)
+        )
     ]
     return found + [diagonal(p)]
 
@@ -85,188 +87,197 @@
     return copy
 
 
-def slab(ref, p, axis, value, gathered, first, rows, core=None):
-    at = {a: (value if a == axis else p[a]) for a in "xyz"}
+def block_of(ref, at, first, rows, core=None):
     every = slice(None)
-    x_lo = every if "x" in gathered else at["x"] % 2
-    x_hi = every if "x" in gathered else at["x"] // 2
-    y = every if "y" in gathered else at["y"]
-    z = every if "z" in gathered else at["z"]
+    where = (at["x"] % 2,) + (() if core is None else (core,)) + (at["y"], at["x"] // 2, at["z"], pl.ds(first, rows), every)
+    return ref.at[where]
+
+
+def unit_of(ref, at, axis, first, rows, core=None):
+    every = slice(None)
+    x_lo, x_hi = (every, every) if axis == "x" else (at["x"] % 2, at["x"] // 2)
+    y = every if axis == "y" else at["y"]
+    z = every if axis == "z" else at["z"]
     where = (x_lo,) + (() if core is None else (core,)) + (y, x_hi, z, pl.ds(first, rows), every)
     return ref.at[where]
 
 
-def halves(first, rows):
-    top = rows // 32 * 16 + (16 if rows % 32 else 0)
-    return ((first, top), (first + top, rows - top))
-
-
-def gather_steps(lanes, w_ref, p, sems):
-    ring_send, ring_recv, sib_send, sib_recv = sems
+def unit_shape(axis, rows):
+    return ((2, 2) if axis == "x" else (4,)) + (rows, 128)
+
+
+AWAY = (0, 1, 2, 1)
+OFFSETS = [(j, k) for j in range(4) for k in range(4)]
+
+
+def depth(offset):
+    return AWAY[offset[0]] + AWAY[offset[1]]
+
+
+def way_two(lane):
+    return 1 if lane % 2 == 0 else 3
+
+
+def way_three(j):
+    return 1 if j % 2 == 0 else 3
+
+
+def onward(lane, offset):
+    j, k = offset
+    to = []
+    if k == 0:
+        to += [(2, 1), (2, 3)]
+        if j == 0:
+            to += [(1, 1), (1, 3)]
+        elif j == way_two(lane):
+            to += [(1, j)]
+    elif k == way_three(j):
+        to += [(2, k)]
+    return to
+
+
+def after(offset, axis_number, by):
+    j, k = offset
+    return ((j + by) % 4, k) if axis_number == 1 else (j, (k + by) % 4)
+
+
+def source(p, order, offset):
+    return moved(moved(p, order[1], 4 - offset[0]), order[2], 4 - offset[1])
+
+
+def wait_bytes(ref, sem):
+    pltpu.make_async_copy(ref, ref, sem).wait()
+
+
+def gather_steps(lanes, w_ref, p, sems, shares):
+    line_send, line_recv, unit_send, unit_recv, sib_send, sib_recv = sems
     core = p["c"]
     sibling = moved(p, "c", 1)
-    pending, to_sibling, passed = [], [], []
-
-    def share(part, lane, i):
-        to_sibling.append(send(part, part, sib_send.at[lane, i], sib_recv.at[lane, i], sibling))
-
-    def arrived(phase):
-        for i, (lane, at, rows, order) in enumerate(lanes):
-            axis, gathered = order[phase], order[:phase]
-            for j in range(2):
-                passed[2 * i + j].wait_recv()
-                if phase == 2:
-                    far = (p[axis] + 2) % 4
-                    share(slab(w_ref, p, axis, far, gathered, *halves(at, rows)[j], core), lane, 3 + j)
-        pending.extend(passed)
-        passed.clear()
-
-    for phase in range(3):
-        if phase:
-            arrived(phase - 1)
-        started = []
+    sent = []
+    lines = []
+    for lane, at, rows, order in lanes:
+        mine = block_of(w_ref, p, at, rows, core)
+        for by in (1, 3, 2):
+            q = moved(p, order[0], by)
+            lines.append(send(mine, mine, line_send.at[lane, by - 1], line_recv.at[lane, by - 1], q))
+    yield
+
+    def pass_on(lane, at, rows, order, offset):
+        unit = unit_of(w_ref, source(p, order, offset), order[0], at, rows, core)
+        for number, by in onward(lane, offset):
+            j, k = after(offset, number, by)
+            sem = lane, j * 4 + k
+            sent.append(send(unit, unit, unit_send.at[sem], unit_recv.at[sem], moved(p, order[number], by)))
+        j, k = offset
+        sem = lane, j * 4 + k
+        shares.append(send(unit, unit, sib_send.at[sem], sib_recv.at[sem], sibling))
+
+    for i, (lane, at, rows, order) in enumerate(lanes):
+        for copy in lines[3 * i : 3 * i + 3]:
+            copy.wait_recv()
+        pass_on(lane, at, rows, order, (0, 0))
+    yield
+    for far in (1, 2, 3, 4):
         for lane, at, rows, order in lanes:
-            axis, gathered = order[phase], order[:phase]
-            mine = slab(w_ref, p, axis, p[axis], gathered, at, rows, core)
-            up, down = moved(p, axis, 1), moved(p, axis, 3)
-            ss, rs = ring_send.at[lane, phase], ring_recv.at[lane, phase]
-            started.append((send(mine, mine, ss.at[0], rs.at[0], up), send(mine, mine, ss.at[1], rs.at[1], down)))
-            if phase == 2:
-                share(mine, lane, 0)
+            for offset in OFFSETS:
+                if depth(offset) == far:
+                    j, k = offset
+                    unit = unit_of(w_ref, source(p, order, offset), order[0], at, rows, core)
+                    pltpu.make_async_remote_copy(
+                        src_ref=unit, dst_ref=unit,
+                        send_sem=unit_send.at[lane, j * 4 + k], recv_sem=unit_recv.at[lane, j * 4 + k],
+                        device_id=device_of(sibling), device_id_type=MESH,
+                    ).wait_recv()
+                    pass_on(lane, at, rows, order, offset)
         yield
-        for (lane, at, rows, order), (to_up, to_down) in zip(lanes, started):
-            axis, gathered = order[phase], order[:phase]
-            up, down = moved(p, axis, 1), moved(p, axis, 3)
-            ss, rs = ring_send.at[lane, phase], ring_recv.at[lane, phase]
-            low, high = halves(at, rows)
-            to_up.wait_recv()
-            part = slab(w_ref, p, axis, down[axis], gathered, *low, core)
-            passed.append(send(part, part, ss.at[2], rs.at[2], up))
-            to_down.wait_recv()
-            part = slab(w_ref, p, axis, up[axis], gathered, *high, core)
-            passed.append(send(part, part, ss.at[3], rs.at[3], down))
-            if phase == 2:
-                for i, q in ((1, down), (2, up)):
-                    share(slab(w_ref, p, axis, q[axis], gathered, at, rows, core), lane, i)
-            pending.extend([to_up, to_down])
-        yield
-    arrived(2)
-    for copy in to_sibling:
+    for copy in shares:
         copy.wait_recv()
-    for copy in pending + to_sibling:
+    for copy in lines + sent + shares:
         copy.wait_send()
     yield
 
 
-def slab_shape(gathered, rows):
-    x = (2,) if "x" in gathered else ()
-    y = (4,) if "y" in gathered else ()
-    z = (4,) if "z" in gathered else ()
-    return x + y + x + z + (rows, 128)
-
-
-def add_blocks(acc, p, axis, value, gathered, first, rows, terms):
-    sizes = slab_shape(gathered, rows)[:-2]
-    count = 1
-    for n in sizes:
-        count *= n
-
+def add_unit(acc, p, at, axis, first, rows, terms):
     def step(i, _):
-        index = []
-        rest = i
-        for n in reversed(sizes):
-            index.append(rest % n)
-            rest = rest // n
-        index = index[::-1]
-        at = iter(index)
-        x_lo = next(at) if "x" in gathered else (value if axis == "x" else p["x"]) % 2
-        y = next(at) if "y" in gathered else (value if axis == "y" else p["y"])
-        x_hi = next(at) if "x" in gathered else (value if axis == "x" else p["x"]) // 2
-        z = next(at) if "z" in gathered else (value if axis == "z" else p["z"])
-        target = (x_lo, p["c"], y, x_hi, z, pl.ds(first, rows), slice(None))
-        total = acc[target].astype(f32)
+        q = dict(at)
+        q[axis] = i
+        target = (q["x"] % 2, p["c"], q["y"], q["x"] // 2, q["z"], pl.ds(first, rows), slice(None))
+        where = (i % 2, i // 2) if axis == "x" else (i,)
+        total = acc[target]
         for term in terms:
-            total = total + term[tuple(index)].astype(f32)
-        acc[target] = total.astype(bf16)
-        return 0
-
-    if count == 1:
-        step(0, 0)
-    else:
-        lax.fori_loop(0, count, step, 0)
-
-
-def reduce_steps(lanes, g_ref, other, bufs, p, sems):
-    ring_send, ring_recv, sib_send, sib_recv = sems
+            total = total + term[where]
+        acc[target] = total
+        return 0
+
+    lax.fori_loop(0, 4, step, 0)
+
+
+def reduce_steps(lanes, g_ref, other, bufs, line_bufs, p, sems):
+    line_send, line_recv, unit_send, unit_recv, sib_send, sib_recv = sems
     core = p["c"]
     sibling = moved(p, "c", 1)
-    pending, from_sibling = [], {}
-    for by in (2, 1, 3, 0):
+    halves, sent = {}, {}
+    for far in (4, 3, 2, 1, 0):
         for lane, at, rows, order in lanes:
-            axis, gathered = order[2], order[:2]
-            value = (p[axis] + by) % 4
-            src = slab(g_ref, p, axis, value, gathered, at, rows, sibling["c"])
-            dst = slab(other, p, axis, value, gathered, at, rows)
-            from_sibling[lane, by] = send(src, dst, sib_send.at[lane, by], sib_recv.at[lane, by], sibling)
+            for offset in OFFSETS:
+                if depth(offset) == far:
+                    where = source(p, order, offset)
+                    src = unit_of(g_ref, where, order[0], at, rows, sibling["c"])
+                    dst = unit_of(other, where, order[0], at, rows)
+                    sem = lane, offset[0] * 4 + offset[1]
+                    halves[lane, offset] = send(src, dst, sib_send.at[sem], sib_recv.at[sem], sibling)
     yield
 
-    def sibling_part(lane, by, axis, gathered, at, rows):
-        from_sibling[lane, by].wait_recv()
-        return slab(other, p, axis, (p[axis] + by) % 4, gathered, at, rows)
-
-    for stage in range(3):
-        phase = 2 - stage
-        one_step = []
+    def add(lane, at, rows, order, offset):
+        halves[lane, offset].wait_recv()
+        where = source(p, order, offset)
+        terms = [unit_of(other, where, order[0], at, rows)]
+        for number, by in onward(lane, offset):
+            child = after(offset, number, by)
+            sent[lane, child].wait_recv()
+            terms.append(bufs[lane].at[child[0] * 4 + child[1] - 1])
+        add_unit(g_ref, p, where, order[0], at, rows, terms)
+
+    def back(lane, at, rows, order, offset):
+        for parent in OFFSETS:
+            for number, by in onward(lane, parent):
+                if after(parent, number, by) == offset:
+                    j, k = offset
+                    sem = lane, j * 4 + k
+                    unit = unit_of(g_ref, source(p, order, offset), order[0], at, rows, core)
+                    sent[lane, offset] = send(
+                        unit, bufs[lane].at[j * 4 + k - 1], unit_send.at[sem], unit_recv.at[sem],
+                        moved(p, order[number], 4 - by),
+                    )
+
+    for far in (4, 3, 2, 1):
         for lane, at, rows, order in lanes:
-            axis, gathered = order[phase], order[:phase]
-            up, down = moved(p, axis, 1), moved(p, axis, 3)
-            far = (p[axis] + 2) % 4
-            b = bufs[lane * 9 + stage * 3]
-            low, high = halves(at, rows)
-            if stage == 0:
-                term = sibling_part(lane, 2, axis, gathered, at, rows)
-                add_blocks(g_ref, p, axis, far, gathered, at, rows, [term])
-            ss, rs = ring_send.at[lane, stage], ring_recv.at[lane, stage]
-            lead = (slice(None),) * (len(b.shape) - 2)
-            low_buf = b.at[lead + (pl.ds(0, low[1]), slice(None))]
-            high_buf = b.at[lead + (pl.ds(low[1], high[1]), slice(None))]
-            one = send(slab(g_ref, p, axis, far, gathered, *low, core), low_buf, ss.at[0], rs.at[0], up)
-            two = send(slab(g_ref, p, axis, far, gathered, *high, core), high_buf, ss.at[1], rs.at[1], down)
-            one_step.append((one, two, low_buf, high_buf))
+            for offset in OFFSETS:
+                if depth(offset) == far:
+                    add(lane, at, rows, order, offset)
+                    back(lane, at, rows, order, offset)
         yield
-        two_step = []
-        for (lane, at, rows, order), (one, two, low_buf, high_buf) in zip(lanes, one_step):
-            axis, gathered = order[phase], order[:phase]
-            up, down = moved(p, axis, 1), moved(p, axis, 3)
-            b = bufs[lane * 9 + stage * 3 : lane * 9 + stage * 3 + 3]
-            low, high = halves(at, rows)
-            ss, rs = ring_send.at[lane, stage], ring_recv.at[lane, stage]
-            if stage == 0:
-                for by, q in ((1, up), (3, down)):
-                    term = sibling_part(lane, by, axis, gathered, at, rows)
-                    add_blocks(g_ref, p, axis, q[axis], gathered, at, rows, [term])
-            one.wait_recv()
-            add_blocks(g_ref, p, axis, up[axis], gathered, *low, [low_buf])
-            three = send(slab(g_ref, p, axis, up[axis], gathered, at, rows, core), b[1], ss.at[2], rs.at[2], up)
-            two.wait_recv()
-            add_blocks(g_ref, p, axis, down[axis], gathered, *high, [high_buf])
-            four = send(slab(g_ref, p, axis, down[axis], gathered, at, rows, core), b[2], ss.at[3], rs.at[3], down)
-            two_step.append((three, four))
-            pending.extend([one, two, three, four])
-        yield
-        for (lane, at, rows, order), (three, four) in zip(lanes, two_step):
-            axis, gathered = order[phase], order[:phase]
-            b = bufs[lane * 9 + stage * 3 : lane * 9 + stage * 3 + 3]
-            terms = [b[1], b[2]]
-            if stage == 0:
-                terms.append(sibling_part(lane, 0, axis, gathered, at, rows))
-            three.wait_recv()
-            four.wait_recv()
-            add_blocks(g_ref, p, axis, p[axis], gathered, at, rows, terms)
-        if stage == 2:
-            for copy in pending + list(from_sibling.values()):
-                copy.wait_send()
-        yield
+    lines = []
+    for lane, at, rows, order in lanes:
+        add(lane, at, rows, order, (0, 0))
+        for by in (1, 3, 2):
+            q = moved(p, order[0], by)
+            src = block_of(g_ref, q, at, rows, core)
+            lines.append(
+                send(src, line_bufs[lane].at[by - 1], line_send.at[lane, by - 1], line_recv.at[lane, by - 1], q)
+            )
+    yield
+    for i, (lane, at, rows, order) in enumerate(lanes):
+        for copy in lines[3 * i : 3 * i + 3]:
+            copy.wait_recv()
+        target = (p["x"] % 2, core, p["y"], p["x"] // 2, p["z"], pl.ds(at, rows), slice(None))
+        total = g_ref[target].astype(f32)
+        for by in range(3):
+            total = total + line_bufs[lane][by].astype(f32)
+        g_ref[target] = total.astype(bf16)
+    for copy in lines + list(sent.values()) + list(halves.values()):
+        copy.wait_send()
+    yield
 
 
 def dot(a, b):
@@ -312,7 +323,7 @@
         )
 
 
-NB = 9 * len(LANES)
+NB = len(LANES)
 
 
 def kernel(
@@ -321,14 +332,14 @@
     out_ref, gx_ref, shard_ref, kv_ref, gn_out,
     *scratch,
 ):
-    bufs, scratch = scratch[:NB], scratch[NB:]
+    bufs, line_bufs, scratch = scratch[:NB], scratch[NB : 2 * NB], scratch[2 * NB :]
     (
         w_ref, g_ref, other, xg, rows_s, s_ref, got, stage,
         cos_ref, sin_ref, wkv, attn_in, attn_in_t, kt, vt, kb, vb, qraw, qb, probs, ctx,
         mlp_in, mlp_in_t, d_b, d_t, act_s, dact_s, hid_s, acc, acc2, dkt, dvt, proj_s,
         dx_got, gn_now, gn_got, final,
-        one_send, one_recv, ring_send, ring_recv, sib_send, sib_recv, x_send, x_recv,
-        back_send, back_recv, bsib_send, bsib_recv, last_send, last_recv, kv_send, kv_recv,
+        one_send, one_recv, line_send, line_recv, unit_send, unit_recv, sib_send, sib_recv, x_send, x_recv,
+        bline_send, bline_recv, back_send, back_recv, bsib_send, bsib_recv, last_send, last_recv, kv_send, kv_recv,
         dx_send, dx_recv, gn_send, gn_recv,
     ) = scratch
     p = place()
@@ -383,14 +394,13 @@
     for copy in first:
         copy.wait_send()
 
-    sems = (ring_send, ring_recv, sib_send, sib_recv)
-    attn = gather_steps(ATTN, w_ref, p, sems)
-    feed = gather_steps(FEED, w_ref, p, sems)
-    for _ in range(2):
-        next(attn), next(feed)
-    for _ in range(2):
-        next(attn), next(feed)
+    sems = (line_send, line_recv, unit_send, unit_recv, sib_send, sib_recv)
+    attn = gather_steps(ATTN, w_ref, p, sems, [])
+    feed = gather_steps(FEED, w_ref, p, sems, [])
     next(attn)
+    for _ in range(3):
+        next(feed)
+        next(attn)
 
     gin, gpa, gpf, gpo, gq, gk = (
         ref[...].reshape(1, ref.shape[0]) for ref in (gin_ref, gpa_ref, gpf_ref, gpo_ref, gq_ref, gk_ref)
@@ -443,8 +453,10 @@
 
     lax.fori_loop(0, 3, input_norm, 0)
     acc[...] = jnp.zeros_like(acc)
+    next(feed)
     next(attn)
     next(feed)
+    next(attn)
     next(attn)
 
     def keyval_in(g, _):
@@ -474,6 +486,7 @@
         return 0
 
     lax.fori_loop(0, 3, keys_values, 0)
+    next(feed)
 
     def head(h, _):
         cos_q, sin_q = cos_ref[2 * PART :, :], sin_ref[2 * PART :, :]
@@ -496,9 +509,7 @@
         acc[...] += dot_nt(c, columns(w_ref, h, 2, 0))
         return 0
 
-    lax.fori_loop(0, 3, head, 0)
-    next(feed)
-    lax.fori_loop(3, 4, head, 0)
+    lax.fori_loop(0, 4, head, 0)
     proj = acc[...]
     proj_s[...] = proj
     mid = x_ref[...].astype(f32) + proj * inv_rms(proj) * gpa
@@ -547,8 +558,8 @@
         return 0
 
     lax.fori_loop(0, 8, feed_back, 0)
-    sems = (back_send, back_recv, bsib_send, bsib_recv)
-    feed = reduce_steps(FEED, g_ref, other, bufs, p, sems)
+    sems = (bline_send, bline_recv, back_send, back_recv, bsib_send, bsib_recv)
+    feed = reduce_steps(FEED, g_ref, other, bufs, line_bufs, p, sems)
     next(feed)
 
     mid = gx_ref[...]
@@ -616,8 +627,9 @@
                     g_ref[tt // 2, tt % 2, 2 * half + yy, g // 4, g % 4, KV0 : KV0 + 32, :] = (
                         stage[20 * tt : 20 * tt + 32, 128 * yy : 128 * yy + 128].astype(bf16)
                     )
-    attn = reduce_steps(ATTN, g_ref, other, bufs, p, sems)
+    attn = reduce_steps(ATTN, g_ref, other, bufs, line_bufs, p, sems)
     next(attn)
+    next(feed)
 
     def input_back(i, extra):
         rows = rows_of(i)
@@ -665,34 +677,12 @@
         gn_now[i + 1] = gn_now[i] + gn_got[i]
 
     gn_start(0)
-    next(attn)
-    next(feed)
-    next(feed)
-    gn_add(0)
-    gn_start(1)
-    next(attn)
-    next(feed)
-    gn_add(1)
-    gn_start(2)
-    next(attn)
-    next(attn)
-    next(feed)
-    next(feed)
-    gn_add(2)
-    gn_start(3)
-    next(attn)
-    next(feed)
-    gn_add(3)
-    gn_start(4)
-    next(attn)
-    next(attn)
-    next(feed)
-    gn_add(4)
-    gn_start(5)
-    next(attn)
-    gn_add(5)
-    gn_start(6)
-    next(attn)
+    for i in range(6):
+        next(attn)
+        if i < 3:
+            next(feed)
+        gn_add(i)
+        gn_start(i + 1)
 
     mine = g_ref[own].astype(f32)
     for i, at in enumerate((0, G0, U0, D0)):
@@ -749,10 +739,8 @@
 def layer(*args):
     dma = pltpu.SemaphoreType.DMA
     vmem = pl.BlockSpec(memory_space=pltpu.VMEM)
-    bufs = []
-    for _, _, rows, order in LANES:
-        for phase in (2, 1, 0):
-            bufs += [pltpu.VMEM(slab_shape(order[:phase], rows), bf16)] * 3
+    bufs = [pltpu.VMEM((15,) + unit_shape(order[0], rows), bf16) for _, _, rows, order in LANES]
+    bufs += [pltpu.VMEM((3, rows, 128), bf16) for _, _, rows, _ in LANES]
     n = len(LANES)
     return pl.pallas_call(
         kernel,
@@ -804,8 +792,10 @@
             pltpu.VMEM((8, 8, D), f32),
             pltpu.VMEM((7, 8, D), f32),
             pltpu.VMEM((4, 24, D), f32),
-            dma((3,)), dma((3,)), dma((n, 3, 4)), dma((n, 3, 4)), dma((n, 5)), dma((n, 5)), dma((2,)), dma((2,)),
-            dma((n, 3, 4)), dma((n, 3, 4)), dma((n, 4)), dma((n, 4)), dma((3,)), dma((3,)), dma((3,)), dma,
+            dma((3,)), dma((3,)), dma((n, 3)), dma((n, 3)), dma((n, 16)), dma((n, 16)), dma((n, 16)), dma((n, 16)),
+            dma((2,)), dma((2,)),
+            dma((n, 3)), dma((n, 3)), dma((n, 16)), dma((n, 16)), dma((n, 16)), dma((n, 16)),
+            dma((3,)), dma((3,)), dma((3,)), dma,
             dma((2,)), dma((2,)), dma((7,)), dma((7,)),
         ],
         compiler_params=pltpu.CompilerParams(

time: 151 us -> 144 us (0.954)
  Pallas kernels: 139 us -> 133 us
    pallas_call x1, Pallas kernels: 139 us -> 133 us  [layer(): pl.pallas_call(kernel, out_shape=(jax.ShapeDtypeStruct((PART, D), bf16),...]
where the time goes in v3:
time: 144 us
  Pallas kernels  133 us (92%)
  local copies, waits for them, and re-layouts  10.5 us (7%)
    pallas_call x1, Pallas kernels, layer(): pl.pallas_call(kernel, out_shape=(jax.ShapeDtypeStruct((PART, D), bf16),...  133 us
    unnamed x28, local copies, waits for them, and re-layouts  6.76 us

profile of v3, /device:TPU:3, one launch (start us, length us, event | category | flops | bytes accessed | tf_op | source)
XLA Modules:
  0.0 144.1 jit_solution(13762395711030306787)
XLA Ops:
  0.6 0.0 copy-start.4
  0.7 1.5 %copy.38.wo_ref = bf16[256,20]{1,0:T(8,128)(2,1)} copy(bf16[256,20]{0,1:T(8,128)(2,1)} %param.23) | data formatting | bytes 20480 | tf_op args[5]
  2.1 0.0 copy-done.4
  2.1 0.8 copy.39.wd_ref
  2.9 132.8 %layer.1 = (bf16[256,640]{1,0:T(8,128)(2,1)}, f32[256,640]{1,0:T(8,128)}, f32[4,24,512]{2,1,0:T(8,128)}, f32[4,24,128]{2,1,0:T(8,128)}, f32[8,640]{1,0:T(8,128)}) custom-call(s32[1,1024]{1,0:T(1,128)} %seg_ref.1, bf16[20,256]{1,0:T(8,128)(2,1)} %wq_ref.1, bf16[20,512]{1,0:T(8,128)(2,1)} %wkv_ref.1, bf16[256,20]{1,0:T(8,128)(2,1)} %copy.38.wo_ref, ...), custom_call_target="tpu_custom_call" | custom-call | tf_op jit(solution)/shard_map/layer/pallas_call | solution.py:745
  135.7 0.0 copy-start.3
  135.7 1.3 fusion.1
  137.1 1.6 %slice_reduce_fusion = (f32[640]{0:T(1024)}, f32[640]{0:T(1024)}, f32[640]{0:T(1024)}, f32[640]{0:T(1024)}) fusion(f32[8,640]{1,0:T(8,128)} %get-tuple-element.23), kind=kLoop, calls=%fused_computation.2 | loop fusion | bytes 20480 | tf_op jit(solution)/shard_map/slice | solution.py:827
  138.6 0.0 copy-start.2
  138.6 0.0 copy-done.3
  138.7 0.6 copy.48
  139.3 0.3 copy-done.2
  139.6 0.1 reshape.52
  139.7 0.1 fusion
  139.8 0.6 copy.51
  140.5 0.6 copy.50
  141.1 0.0 copy-start.1
  141.1 0.0 copy-start
  141.2 0.6 copy.49
  141.9 0.6 slice_bitcast_fusion.1
  142.5 0.0 copy-done.1
  142.5 0.7 copy.54
  143.2 0.0 copy-done
  143.2 0.8 copy.55
  (12 shorter events, 0.2 us)
Async XLA Ops:
  0.6 1.5 %copy-start.4 = (bf16[512,20]{0,1:T(8,128)(2,1)S(1)}, bf16[512,20]{0,1:T(8,128)(2,1)}, u32[]{:S(2)}) copy-start(bf16[512,20]{0,1:T(8,128)(2,1)} %param.26) | copy-start | bytes 61444
  135.7 2.9 %copy-start.3 = (f32[4,24,128]{2,1,0:T(8,128)S(1)}, f32[4,24,128]{2,1,0:T(8,128)}, u32[]{:S(2)}) copy-start(f32[4,24,128]{2,1,0:T(8,128)} %get-tuple-element.22) | copy-start | bytes 147460
  138.6 0.9 copy-start.2
  141.1 1.4 copy-start.1
  141.1 2.1 %copy-start = (f32[256,640]{1,0:T(8,128)S(1)}, f32[256,640]{1,0:T(8,128)}, u32[]{:S(2)}) copy-start(f32[256,640]{1,0:T(8,128)} %get-tuple-element.51) | copy-start | bytes 1966084

commit v4 on v3

--- a/solution.py
+++ b/solution.py
@@ -16,7 +16,7 @@
 GROUPS = 8
 KV0, G0, U0, D0 = 80, 112, 192, 272
 ATTN = ((0, 0, 48, "xyz"), (1, 48, 32, "yzx"), (2, 80, 32, "zxy"))
-FEED = ((3, 112, 80, "xyz"), (4, 192, 80, "yzx"), (5, 272, 80, "zxy"))
+FEED = ((3, 112, 80, "xyz"), (4, 192, 64, "yzx"), (5, 256, 96, "zxy"))
 LANES = ATTN + FEED
 norm_eps = 1e-06
 rope_base = 10000.0
@@ -118,8 +118,8 @@
     return 1 if lane % 2 == 0 else 3
 
 
-def way_three(j):
-    return 1 if j % 2 == 0 else 3
+def way_three(lane, j):
+    return 1 if j % 2 == 0 and lane % 3 != 1 else 3
 
 
 def onward(lane, offset):
@@ -131,7 +131,7 @@
             to += [(1, 1), (1, 3)]
         elif j == way_two(lane):
             to += [(1, j)]
-    elif k == way_three(j):
+    elif k == way_three(lane, j):
         to += [(2, k)]
     return to
 
@@ -351,16 +351,14 @@
     greet(p)
 
     rows_s[...] = jnp.zeros_like(rows_s)
-    out_t = wo_ref[...].astype(f32).T
-    down_t = wd_ref[...].astype(f32).T
     for j in range(4):
         if j < 2:
             rows_s[j, :20, :128] = wq_ref[:, 128 * j : 128 * j + 128].astype(f32)
         else:
-            rows_s[j, :20, :128] = out_t[:, 128 * j - 256 : 128 * j - 128]
+            rows_s[j, :20, :128] = wo_ref[:, 128 * j - 256 : 128 * j - 128].astype(f32)
         rows_s[j, :20, 128:256] = wg_ref[:, 128 * j : 128 * j + 128].astype(f32)
         rows_s[j, :20, 256:384] = wu_ref[:, 128 * j : 128 * j + 128].astype(f32)
-        rows_s[j, :20, 384:512] = down_t[:, 128 * j : 128 * j + 128]
+        rows_s[j, :20, 384:512] = wd_ref[:, 128 * j : 128 * j + 128].astype(f32)
         rows_s[j, :20, 512:] = wkv_ref[:, 128 * j : 128 * j + 128].astype(f32)
     s_ref[...] = rows_s[...].astype(bf16)
     first = []
@@ -648,15 +646,19 @@
     gx_ref[...] += input_back(2, acc[...])
 
     def dx_copy(k):
+        to = jnp.maximum(t - 1, 0) if k == 1 else jnp.where(t == 3, 2, 0)
         return pltpu.make_async_remote_copy(
             src_ref=attn_in.at[2 - k], dst_ref=dx_got.at[k - 1], send_sem=dx_send.at[k - 1], recv_sem=dx_recv.at[k - 1],
-            device_id={"dp": dp, "tensor": jnp.maximum(t - k, 0)}, device_id_type=MESH,
+            device_id={"dp": dp, "tensor": to}, device_id_type=MESH,
         )
 
-    for k in (1, 2):
-        @pl.when(t - k >= 0)
-        def _(k=k):
-            dx_copy(k).start()
+    @pl.when(t >= 2)
+    def _():
+        dx_copy(2).start()
+
+    @pl.when(lax.rem(t, 2) == 1)
+    def _():
+        dx_copy(1).start()
 
     def pair(i):
         if i == 6:
@@ -679,6 +681,13 @@
     gn_start(0)
     for i in range(6):
         next(attn)
+        if i == 0:
+            @pl.when(t == 2)
+            def _():
+                dx_copy(2).wait_recv()
+                attn_in[1] = (attn_in[1].astype(f32) + dx_got[1].astype(f32)).astype(bf16)
+                dx_copy(1).start()
+
         if i < 3:
             next(feed)
         gn_add(i)
@@ -697,15 +706,24 @@
     final[pl.ds(y, 1)] = rows_s[pl.ds(y, 1), :24]
     gn_add(6)
     gn_out[...] = gn_now[7]
-    for k in (1, 2):
-        @pl.when(t + k <= 3)
-        def _(k=k):
-            dx_copy(k).wait_recv()
-            gx_ref[...] += dx_got[k - 1].astype(f32)
-
-        @pl.when(t - k >= 0)
-        def _(k=k):
-            dx_copy(k).wait_send()
+
+    @pl.when(t < 3)
+    def _():
+        dx_copy(1).wait_recv()
+        gx_ref[...] += dx_got[0].astype(f32)
+
+    @pl.when(t == 0)
+    def _():
+        dx_copy(2).wait_recv()
+        gx_ref[...] += dx_got[1].astype(f32)
+
+    @pl.when(t >= 1)
+    def _():
+        dx_copy(1).wait_send()
+
+    @pl.when(t >= 2)
+    def _():
+        dx_copy(2).wait_send()
 
     for copy in last:
         copy.wait_recv()
@@ -805,6 +823,40 @@
     )(*args)
 
 
+def finish_kernel(
+    out_ref, gx_ref, shard_ref, kv_ref, gn_ref,
+    out_to, gx_to, query_to, keyval_to, out_t_to, gate_to, up_to, down_t_to, *gains_to,
+):
+    out_to[...] = out_ref[...]
+    gx_to[...] = gx_ref[...]
+    for j in range(4):
+        here = slice(128 * j, 128 * j + 128)
+        if j < 2:
+            query_to[:, here] = shard_ref[j, :20, :128]
+        else:
+            out_t_to[:, 128 * j - 256 : 128 * j - 128] = shard_ref[j, :20, :128]
+        gate_to[:, here] = shard_ref[j, :20, 128:256]
+        up_to[:, here] = shard_ref[j, :20, 256:384]
+        down_t_to[:, here] = shard_ref[j, :20, 384:512]
+        keyval_to[:, here] = kv_ref[j, :20, :]
+    for i, ref in enumerate(gains_to):
+        ref[...] = gn_ref[i : i + 1, : ref.shape[0]].reshape(ref.shape[0])
+
+
+def finish(*args):
+    vmem = pl.BlockSpec(memory_space=pltpu.VMEM)
+    shapes = [((PART, D), bf16), ((PART, D), f32)]
+    shapes += [((20, n), f32) for n in (256, 512, 256, 512, 512, 512)]
+    shapes += [((n,), f32) for n in (D, D, D, D, HD, HD)]
+    return pl.pallas_call(
+        finish_kernel,
+        out_shape=tuple(jax.ShapeDtypeStruct(*item) for item in shapes),
+        in_specs=[vmem] * len(args),
+        out_specs=(vmem,) * len(shapes),
+        name="finish",
+    )(*args)
+
+
 def rope_parts():
     freq = (rope_base ** (-np.arange(0, HD, 2, dtype=np.float64) / HD))[None, :]
     angles = np.arange(KEYS, dtype=np.float64)[:, None] * freq
@@ -815,17 +867,12 @@
     tokens, segments, cotangent, w_query, w_keyval, w_out, w_gate, w_up, w_down,
     gain_in, gain_post_attn, gain_pre_ff, gain_post_ff, gain_query, gain_key,
 ):
-    output, grad_x, shard, kv, gn = layer(
-        segments, w_query, w_keyval, w_out, w_gate, w_up, w_down, tokens, cotangent,
+    made = layer(
+        segments, w_query, w_keyval, w_out.T, w_gate, w_up, w_down.T, tokens, cotangent,
         gain_in, gain_post_attn, gain_pre_ff, gain_post_ff, gain_query, gain_key, *rope_parts(),
     )
-    rows = shard[:, :20].reshape(4, 20, 4, 128)
-    first, gate, up, down = (jnp.moveaxis(rows[:, :, i], 0, 1).reshape(20, 512) for i in range(4))
-    grad_kv = jnp.moveaxis(kv[:, :20], 0, 1).reshape(20, 512)
-    return (
-        output, grad_x, first[:, :256], grad_kv, first[:, 256:].T, gate, up, down.T,
-        gn[0], gn[1], gn[2], gn[3], gn[4, :HD], gn[5, :HD],
-    )
+    output, grad_x, query, keyval, out_t, gate, up, down_t, *gains = finish(*made)
+    return (output, grad_x, query, keyval, out_t.T, gate, up, down_t.T, *gains)
 
 
 def solution(mesh):

time: 144 us -> 130 us (0.903)
  local copies, waits for them, and re-layouts: 10.5 us -> 0 us
  Pallas kernels: 133 us -> 129 us
    unnamed x28 -> x0, local copies, waits for them, and re-layouts: 6.76 us -> none
    pallas_call x1, Pallas kernels: 133 us -> 126 us  [layer(): pl.pallas_call(kernel, out_shape=(jax.ShapeDtypeStruct((PART, D), bf16),...]
    slice x3 -> x0, local copies, waits for them, and re-layouts: 3.04 us -> none  [the longest x1 1.58 us: per_device(): gn[3]]
    pallas_call x0 -> x1, Pallas kernels: none -> 2.35 us  [finish(): pl.pallas_call(finish_kernel, out_shape=tuple((jax.ShapeDtypeStruct(*item...]
where the time goes in v4:
time: 130 us
  Pallas kernels  129 us (99%)
    pallas_call x1, Pallas kernels, layer(): pl.pallas_call(kernel, out_shape=(jax.ShapeDtypeStruct((PART, D), bf16),...  126 us

profile of v4, /device:TPU:3, one launch (start us, length us, event | category | flops | bytes accessed | tf_op | source)
XLA Modules:
  0.0 129.6 jit_solution(9855197976972035752)
XLA Ops:
  0.7 126.4 %layer.1 = (bf16[256,640]{1,0:T(8,128)(2,1)}, f32[256,640]{1,0:T(8,128)}, f32[4,24,512]{2,1,0:T(8,128)}, f32[4,24,128]{2,1,0:T(8,128)}, f32[8,640]{1,0:T(8,128)}) custom-call(s32[1,1024]{1,0:T(1,128)} %seg_ref.1, bf16[20,256]{1,0:T(8,128)(2,1)} %wq_ref.1, bf16[20,512]{1,0:T(8,128)(2,1)} %wkv_ref.1, bf16[20,256]{1,0:T(8,128)(2,1)} %bitcast.5, ...), custom_call_target="tpu_custom_call" | custom-call | tf_op jit(solution)/shard_map/layer/pallas_call | solution.py:763
  127.1 2.3 %finish.1 = (bf16[256,640]{1,0:T(8,128)(2,1)}, f32[256,640]{1,0:T(8,128)}, f32[20,256]{1,0:T(8,128)}, f32[20,512]{1,0:T(8,128)}, f32[20,256]{1,0:T(8,128)}, /*in...) custom-call(bf16[256,640]{1,0:T(8,128)(2,1)} %get-tuple-element.33.o, ...), custom_call_target="tpu_custom_call" | custom-call | tf_op jit(solution)/shard_map/finish/pallas_call | solution.py:851

commit v5 on v4

--- a/solution.py
+++ b/solution.py
@@ -66,12 +66,20 @@
     return found + [diagonal(p)]
 
 
-def greet(p):
+def say_here(p, t):
     barrier = pltpu.get_barrier_semaphore()
-    peers = peers_of(p)
-    for q in peers:
+    for q in peers_of(p):
         pl.semaphore_signal(barrier, inc=1, device_id=device_of(q), device_id_type=MESH)
-    pl.semaphore_wait(barrier, len(peers))
+    for y in range(4):
+        @pl.when((t != p["y"]) | (y != p["y"]))
+        def _(y=y):
+            there = {"dp": lax.axis_index("dp") - p["y"] + y, "tensor": p["y"]}
+            pl.semaphore_signal(barrier, inc=1, device_id=there, device_id_type=MESH)
+
+
+def all_here(p, t):
+    barrier = pltpu.get_barrier_semaphore()
+    pl.semaphore_wait(barrier, len(peers_of(p)) + jnp.where(t == p["y"], 3, 4))
 
 
 def send(src, dst, send_sem, recv_sem, q):
@@ -209,7 +217,7 @@
         acc[target] = total
         return 0
 
-    lax.fori_loop(0, 4, step, 0)
+    lax.fori_loop(0, 4, step, 0, unroll=rows < 64)
 
 
 def reduce_steps(lanes, g_ref, other, bufs, line_bufs, p, sems):
@@ -348,7 +356,7 @@
     y = p["y"]
     core = p["c"]
     own = (p["x"] % 2, core, y, p["x"] // 2, p["z"])
-    greet(p)
+    say_here(p, t)
 
     rows_s[...] = jnp.zeros_like(rows_s)
     for j in range(4):
@@ -361,45 +369,6 @@
         rows_s[j, :20, 384:512] = wd_ref[:, 128 * j : 128 * j + 128].astype(f32)
         rows_s[j, :20, 512:] = wkv_ref[:, 128 * j : 128 * j + 128].astype(f32)
     s_ref[...] = rows_s[...].astype(bf16)
-    first = []
-    for k in (1, 3, 2):
-        q = moved(p, "y", k)
-        first.append(send(s_ref.at[q["y"]], got.at[y], one_send.at[k - 1], one_recv.at[k - 1], q))
-
-    def token_copy(src, slot, to):
-        return pltpu.make_async_remote_copy(
-            src_ref=src, dst_ref=xg.at[slot], send_sem=x_send.at[1 - slot], recv_sem=x_recv.at[1 - slot],
-            device_id={"dp": dp, "tensor": to}, device_id_type=MESH,
-        )
-
-    @pl.when(t < 3)
-    def _():
-        token_copy(x_ref, 1, jnp.minimum(t + 1, 3)).start()
-
-    @pl.when(t == 0)
-    def _():
-        token_copy(x_ref, 0, t + 2).start()
-
-    xg[2] = x_ref[...]
-    got[pl.ds(y, 1)] = s_ref[pl.ds(y, 1)]
-    for copy in first:
-        copy.wait_recv()
-    for j in range(4):
-        stage[20 * j : 20 * j + 20, :] = got[j].astype(f32)[:20, :512]
-    for i, at in enumerate((0, G0, U0, D0)):
-        w_ref[own + (slice(at, at + 80),)] = stage[:80, 128 * i : 128 * i + 128].astype(bf16)
-    w_ref[own + (slice(KV0, KV0 + 32),)] = got[pl.ds(t, 1)][0, :, 512:640]
-    for copy in first:
-        copy.wait_send()
-
-    sems = (line_send, line_recv, unit_send, unit_recv, sib_send, sib_recv)
-    attn = gather_steps(ATTN, w_ref, p, sems, [])
-    feed = gather_steps(FEED, w_ref, p, sems, [])
-    next(attn)
-    for _ in range(3):
-        next(feed)
-        next(attn)
-
     gin, gpa, gpf, gpo, gq, gk = (
         ref[...].reshape(1, ref.shape[0]) for ref in (gin_ref, gpa_ref, gpf_ref, gpo_ref, gq_ref, gk_ref)
     )
@@ -419,6 +388,46 @@
     cos_ref[...] = ca * cd + sa * sd
     sin_ref[...] = sa * cd - ca * sd
 
+    xg[2] = x_ref[...]
+    got[pl.ds(y, 1)] = s_ref[pl.ds(y, 1)]
+    all_here(p, t)
+    first = []
+    for k in (1, 3, 2):
+        q = moved(p, "y", k)
+        first.append(send(s_ref.at[q["y"]], got.at[y], one_send.at[k - 1], one_recv.at[k - 1], q))
+
+    def token_copy(src, slot, to):
+        return pltpu.make_async_remote_copy(
+            src_ref=src, dst_ref=xg.at[slot], send_sem=x_send.at[1 - slot], recv_sem=x_recv.at[1 - slot],
+            device_id={"dp": dp, "tensor": to}, device_id_type=MESH,
+        )
+
+    @pl.when(t < 3)
+    def _():
+        token_copy(x_ref, 1, jnp.minimum(t + 1, 3)).start()
+
+    @pl.when(t == 0)
+    def _():
+        token_copy(x_ref, 0, t + 2).start()
+
+    for copy in first:
+        copy.wait_recv()
+    for j in range(4):
+        stage[20 * j : 20 * j + 20, :] = got[j].astype(f32)[:20, :512]
+    for i, at in enumerate((0, G0, U0, D0)):
+        w_ref[own + (slice(at, at + 80),)] = stage[:80, 128 * i : 128 * i + 128].astype(bf16)
+    w_ref[own + (slice(KV0, KV0 + 32),)] = got[pl.ds(t, 1)][0, :, 512:640]
+    for copy in first:
+        copy.wait_send()
+
+    sems = (line_send, line_recv, unit_send, unit_recv, sib_send, sib_recv)
+    attn = gather_steps(ATTN, w_ref, p, sems, [])
+    feed = gather_steps(FEED, w_ref, p, sems, [])
+    next(attn)
+    for _ in range(5):
+        next(feed)
+        next(attn)
+
     @pl.when(t > 0)
     def _():
         token_copy(x_ref, 1, jnp.minimum(t + 1, 3)).wait_recv()
@@ -451,10 +460,6 @@
 
     lax.fori_loop(0, 3, input_norm, 0)
     acc[...] = jnp.zeros_like(acc)
-    next(feed)
-    next(attn)
-    next(feed)
-    next(attn)
     next(attn)
 
     def keyval_in(g, _):
@@ -699,6 +704,25 @@
             rows_s[j, 0:20, 128 * i : 128 * i + 128] = mine[at + 20 * j : at + 20 * j + 20]
     for j in range(4):
         rows_s[j, :24, 512:] = mine[KV0 : KV0 + 24]
+
+    @pl.when(t == y)
+    def _():
+        kv_ref[pl.ds(y, 1)] = mine[KV0 : KV0 + 24][None]
+
+
+    def kv_copy(k):
+        return pltpu.make_async_remote_copy(
+            src_ref=rows_s.at[0, pl.ds(0, 24), pl.ds(512, 128)], dst_ref=kv_ref.at[y],
+            send_sem=kv_send.at[k], recv_sem=kv_recv.at[y],
+            device_id={"dp": dp - y + t, "tensor": (t + k) % 4}, device_id_type=MESH,
+        )
+
+    @pl.when(t != y)
+    def _():
+        kv_copy(0).start()
+
+    for k in (1, 2, 3):
+        kv_copy(k).start()
     last = []
     for k in (1, 3, 2):
         q = moved(p, "y", k)
@@ -728,30 +752,24 @@
     for copy in last:
         copy.wait_recv()
 
-    def kv_copy(k):
-        return pltpu.make_async_remote_copy(
-            src_ref=final.at[:, :, pl.ds(512, 128)], dst_ref=kv_ref, send_sem=kv_send.at[k - 1], recv_sem=kv_recv,
-            device_id={"dp": dp, "tensor": (t + k) % 4}, device_id_type=MESH,
-        )
-
-    @pl.when(t == y)
-    def _():
-        for k in (1, 2, 3):
-            kv_copy(k).start()
-        kv_ref[...] = final[:, :, 512:640]
-
     shard_ref[...] = final[:, :, :512]
     for copy in gn_copies + last:
         copy.wait_send()
 
-    @pl.when(t == y)
-    def _():
-        for k in (1, 2, 3):
-            kv_copy(k).wait_send()
+    for k in (1, 2, 3):
+        kv_copy(k).wait_send()
 
     @pl.when(t != y)
     def _():
-        kv_copy(1).wait_recv()
+        kv_copy(0).wait_send()
+
+    for j in range(4):
+        @pl.when((t != y) | (y != j))
+        def _(j=j):
+            pltpu.make_async_remote_copy(
+                src_ref=kv_ref.at[j], dst_ref=kv_ref.at[j], send_sem=kv_send.at[0], recv_sem=kv_recv.at[j],
+                device_id={"dp": dp, "tensor": (t + 1) % 4}, device_id_type=MESH,
+            ).wait_recv()
 
 
 def layer(*args):
@@ -813,7 +831,7 @@
             dma((3,)), dma((3,)), dma((n, 3)), dma((n, 3)), dma((n, 16)), dma((n, 16)), dma((n, 16)), dma((n, 16)),
             dma((2,)), dma((2,)),
             dma((n, 3)), dma((n, 3)), dma((n, 16)), dma((n, 16)), dma((n, 16)), dma((n, 16)),
-            dma((3,)), dma((3,)), dma((3,)), dma,
+            dma((3,)), dma((3,)), dma((4,)), dma((4,)),
             dma((2,)), dma((2,)), dma((7,)), dma((7,)),
         ],
         compiler_params=pltpu.CompilerParams(

time: 130 us -> 129 us (level)
  Pallas kernels: 129 us -> 127 us
    pallas_call x1, Pallas kernels: 126 us -> 125 us  [layer(): pl.pallas_call(kernel, out_shape=(jax.ShapeDtypeStruct((PART, D), bf16),...]
where the time goes in v5:
time: 129 us; the launch traced here: 128 us
  Pallas kernels  127 us (98%)
    pallas_call x1, Pallas kernels, layer(): pl.pallas_call(kernel, out_shape=(jax.ShapeDtypeStruct((PART, D), bf16),...  125 us

profile of v5, /device:TPU:3, one launch (start us, length us, event | category | flops | bytes accessed | tf_op | source)
XLA Modules:
  0.0 128.2 jit_solution(11003952986196203633)
XLA Ops:
  0.7 125.0 %layer.1 = (bf16[256,640]{1,0:T(8,128)(2,1)}, f32[256,640]{1,0:T(8,128)}, f32[4,24,512]{2,1,0:T(8,128)}, f32[4,24,128]{2,1,0:T(8,128)}, f32[8,640]{1,0:T(8,128)}) custom-call(s32[1,1024]{1,0:T(1,128)} %seg_ref.1, bf16[20,256]{1,0:T(8,128)(2,1)} %wq_ref.1, bf16[20,512]{1,0:T(8,128)(2,1)} %wkv_ref.1, bf16[20,256]{1,0:T(8,128)(2,1)} %bitcast.5, ...), custom_call_target="tpu_custom_call" | custom-call | tf_op jit(solution)/shard_map/layer/pallas_call | solution.py:781
  125.7 2.3 %finish.1 = (bf16[256,640]{1,0:T(8,128)(2,1)}, f32[256,640]{1,0:T(8,128)}, f32[20,256]{1,0:T(8,128)}, f32[20,512]{1,0:T(8,128)}, f32[20,256]{1,0:T(8,128)}, /*in...) custom-call(bf16[256,640]{1,0:T(8,128)(2,1)} %get-tuple-element.33.o, ...), custom_call_target="tpu_custom_call" | custom-call | tf_op jit(solution)/shard_map/finish/pallas_call | solution.py:869

commit v6 on v5

--- a/solution.py
+++ b/solution.py
@@ -217,7 +217,7 @@
         acc[target] = total
         return 0
 
-    lax.fori_loop(0, 4, step, 0, unroll=rows < 64)
+    lax.fori_loop(0, 4, step, 0, unroll=True)
 
 
 def reduce_steps(lanes, g_ref, other, bufs, line_bufs, p, sems):

time: 129 us -> 129 us (level)
  no operation moved by 1% of the time
where the time goes in v6:
time: 129 us; the launch traced here: 128 us
  Pallas kernels  127 us (98%)
    pallas_call x1, Pallas kernels, layer(): pl.pallas_call(kernel, out_shape=(jax.ShapeDtypeStruct((PART, D), bf16),...  125 us

profile of v6, /device:TPU:3, one launch (start us, length us, event | category | flops | bytes accessed | tf_op | source)
XLA Modules:
  0.0 127.9 jit_solution(1880534202684685204)
XLA Ops:
  0.7 124.7 %layer.1 = (bf16[256,640]{1,0:T(8,128)(2,1)}, f32[256,640]{1,0:T(8,128)}, f32[4,24,512]{2,1,0:T(8,128)}, f32[4,24,128]{2,1,0:T(8,128)}, f32[8,640]{1,0:T(8,128)}) custom-call(s32[1,1024]{1,0:T(1,128)} %seg_ref.1, bf16[20,256]{1,0:T(8,128)(2,1)} %wq_ref.1, bf16[20,512]{1,0:T(8,128)(2,1)} %wkv_ref.1, bf16[20,256]{1,0:T(8,128)(2,1)} %bitcast.5, ...), custom_call_target="tpu_custom_call" | custom-call | tf_op jit(solution)/shard_map/layer/pallas_call | solution.py:781
  125.3 2.3 %finish.1 = (bf16[256,640]{1,0:T(8,128)(2,1)}, f32[256,640]{1,0:T(8,128)}, f32[20,256]{1,0:T(8,128)}, f32[20,512]{1,0:T(8,128)}, f32[20,256]{1,0:T(8,128)}, /*in...) custom-call(bf16[256,640]{1,0:T(8,128)(2,1)} %get-tuple-element.33.o, ...), custom_call_target="tpu_custom_call" | custom-call | tf_op jit(solution)/shard_map/finish/pallas_call | solution.py:869

commit v7 on v6

--- a/solution.py
+++ b/solution.py
@@ -633,6 +633,7 @@
     attn = reduce_steps(ATTN, g_ref, other, bufs, line_bufs, p, sems)
     next(attn)
     next(feed)
+    next(attn)
 
     def input_back(i, extra):
         rows = rows_of(i)
@@ -648,8 +649,6 @@
 
     gn_now[0, 0:1, :] = jnp.zeros((1, D), f32)
     lax.fori_loop(0, 2, input_back_before, 0)
-    gx_ref[...] += input_back(2, acc[...])
-
     def dx_copy(k):
         to = jnp.maximum(t - 1, 0) if k == 1 else jnp.where(t == 3, 2, 0)
         return pltpu.make_async_remote_copy(
@@ -665,26 +664,31 @@
     def _():
         dx_copy(1).start()
 
-    def pair(i):
-        if i == 6:
-            return moved(p, "c", 1)
-        axis = "xyz"[i // 2]
-        m = p[axis]
-        q = dict(p)
-        q[axis] = (m // 2) * 2 + (1 - m % 2) if i % 2 == 0 else 3 - m
-        return q
-
-    gn_copies = []
+    gn_copies = [[], [], [], []]
 
     def gn_start(i):
-        gn_copies.append(send(gn_now.at[i], gn_got.at[i], gn_send.at[i], gn_recv.at[i], pair(i)))
+        if i == 3:
+            gn_copies[3].append(send(gn_now.at[3], gn_got.at[12], gn_send.at[9], gn_recv.at[9], moved(p, "c", 1)))
+            return
+        axis = "xyz"[i]
+        gn_got[pl.ds(4 * i + p[axis], 1)] = gn_now[i][None]
+        for by in (1, 3, 2):
+            sem = 3 * i + by - 1
+            dst = gn_got.at[4 * i + p[axis]]
+            gn_copies[i].append(send(gn_now.at[i], dst, gn_send.at[sem], gn_recv.at[sem], moved(p, axis, by)))
 
     def gn_add(i):
-        gn_copies[i].wait_recv()
-        gn_now[i + 1] = gn_now[i] + gn_got[i]
-
+        for copy in gn_copies[i]:
+            copy.wait_recv()
+        if i == 3:
+            gn_now[4] = gn_now[3] + gn_got[12]
+        else:
+            gn_now[i + 1] = (gn_got[4 * i] + gn_got[4 * i + 1]) + (gn_got[4 * i + 2] + gn_got[4 * i + 3])
+
+    next(attn)
+    gx_ref[...] += input_back(2, acc[...])
     gn_start(0)
-    for i in range(6):
+    for i in range(4):
         next(attn)
         if i == 0:
             @pl.when(t == 2)
@@ -695,8 +699,8 @@
 
         if i < 3:
             next(feed)
-        gn_add(i)
-        gn_start(i + 1)
+            gn_add(i)
+            gn_start(i + 1)
 
     mine = g_ref[own].astype(f32)
     for i, at in enumerate((0, G0, U0, D0)):
@@ -728,8 +732,8 @@
         q = moved(p, "y", k)
         last.append(send(rows_s.at[q["y"], pl.ds(0, 24), :], final.at[y], last_send.at[k - 1], last_recv.at[k - 1], q))
     final[pl.ds(y, 1)] = rows_s[pl.ds(y, 1), :24]
-    gn_add(6)
-    gn_out[...] = gn_now[7]
+    gn_add(3)
+    gn_out[...] = gn_now[4]
 
     @pl.when(t < 3)
     def _():
@@ -753,7 +757,7 @@
         copy.wait_recv()
 
     shard_ref[...] = final[:, :, :512]
-    for copy in gn_copies + last:
+    for copy in sum(gn_copies, last):
         copy.wait_send()
 
     for k in (1, 2, 3):
@@ -825,14 +829,14 @@
             pltpu.VMEM((HD, KEYS), f32),
             pltpu.VMEM((PART, D), f32),
             pltpu.VMEM((2, PART, D), bf16),
-            pltpu.VMEM((8, 8, D), f32),
-            pltpu.VMEM((7, 8, D), f32),
+            pltpu.VMEM((5, 8, D), f32),
+            pltpu.VMEM((13, 8, D), f32),
             pltpu.VMEM((4, 24, D), f32),
             dma((3,)), dma((3,)), dma((n, 3)), dma((n, 3)), dma((n, 16)), dma((n, 16)), dma((n, 16)), dma((n, 16)),
             dma((2,)), dma((2,)),
             dma((n, 3)), dma((n, 3)), dma((n, 16)), dma((n, 16)), dma((n, 16)), dma((n, 16)),
             dma((3,)), dma((3,)), dma((4,)), dma((4,)),
-            dma((2,)), dma((2,)), dma((7,)), dma((7,)),
+            dma((2,)), dma((2,)), dma((10,)), dma((10,)),
         ],
         compiler_params=pltpu.CompilerParams(
             collective_id=0, has_side_effects=True, vmem_limit_bytes=62 << 20

time: 129 us -> 126 us (0.977)
  Pallas kernels: 127 us -> 124 us
    pallas_call x1, Pallas kernels: 125 us -> 121 us  [layer(): pl.pallas_call(kernel, out_shape=(jax.ShapeDtypeStruct((PART, D), bf16),...]
where the time goes in v7:
time: 126 us; the launch traced here: 125 us
  Pallas kernels  124 us (98%)
    pallas_call x1, Pallas kernels, layer(): pl.pallas_call(kernel, out_shape=(jax.ShapeDtypeStruct((PART, D), bf16),...  121 us

profile of v7, /device:TPU:3, one launch (start us, length us, event | category | flops | bytes accessed | tf_op | source)
XLA Modules:
  0.0 124.6 jit_solution(15210764285520018360)
XLA Ops:
  0.7 121.4 %layer.1 = (bf16[256,640]{1,0:T(8,128)(2,1)}, f32[256,640]{1,0:T(8,128)}, f32[4,24,512]{2,1,0:T(8,128)}, f32[4,24,128]{2,1,0:T(8,128)}, f32[8,640]{1,0:T(8,128)}) custom-call(s32[1,1024]{1,0:T(1,128)} %seg_ref.1, bf16[20,256]{1,0:T(8,128)(2,1)} %wq_ref.1, bf16[20,512]{1,0:T(8,128)(2,1)} %wkv_ref.1, bf16[20,256]{1,0:T(8,128)(2,1)} %bitcast.5, ...), custom_call_target="tpu_custom_call" | custom-call | tf_op jit(solution)/shard_map/layer/pallas_call | solution.py:785
  122.1 2.3 %finish.1 = (bf16[256,640]{1,0:T(8,128)(2,1)}, f32[256,640]{1,0:T(8,128)}, f32[20,256]{1,0:T(8,128)}, f32[20,512]{1,0:T(8,128)}, f32[20,256]{1,0:T(8,128)}, /*in...) custom-call(bf16[256,640]{1,0:T(8,128)(2,1)} %get-tuple-element.33.o, ...), custom_call_target="tpu_custom_call" | custom-call | tf_op jit(solution)/shard_map/finish/pallas_call | solution.py:873
